TPU v7x, 32 devices: a whole 2x2x4 slice. The times are simulated.
32 devices in a mesh: dp: 2 (over x), seq: 4 (over z), tensor: 4 (over y, core).
Axes of the slice: x: 2, y: 2, z: 4, core: 2. Of those that a mesh axis runs over, the one named last changes fastest.
Arguments:
- x_in: bfloat16 [2, 2048, 768], P('dp', 'seq'), may hold values from -6 to 6
- cotangent: bfloat16 [2, 2048, 768], P('dp', 'seq'), may hold values from -6 to 6
- segment_ids: int32 [2, 2048], P('dp'), may hold values from 0 to 31, never falling along the last dimension, each value on 1 to 1600 neighbouring positions
- random_blocks: int32 [2, 12, 32, 3], P('dp', 'tensor'), may hold values from 1 to 30, as said below
- query_key_value_weight: float32 [2, 768, 3, 768], P(None, ('dp', 'seq'), None, 'tensor'), may hold values from -0.21875 to 0.21875
- mixer_exit_projection_matrix: float32 [2, 768, 768], P(None, 'tensor', ('dp', 'seq')), may hold values from -2.5 to 2.5
- ffn_input_weight: float32 [2, 768, 3072], P(None, ('dp', 'seq'), 'tensor'), may hold values from -0.21875 to 0.21875
- perceptron_exit_matrix: float32 [2, 3072, 768], P(None, 'tensor', ('dp', 'seq')), may hold values from -0.15625 to 0.15625
- qv_bias: float32 [2, 2, 4, 192], P(None, None, 'tensor', ('dp', 'seq')), may hold values from -4 to 4
- mid_bias: float32 [2, 4, 768], P(None, 'tensor', ('dp', 'seq')), may hold values from -4 to 4
- shifts: float32 [2, 4, 768], P(None, None, ('dp', 'seq')), may hold values from -4 to 4
- gains: float32 [2, 2, 768], P(None, None, ('dp', 'seq')), may hold values from 0.5 to 1.5
Outputs:
- activations: bfloat16 [2, 2048, 768], P('dp', 'seq')
- input_grad: float32 [2, 2048, 768], P('dp', 'seq')
- derivative_joint_projection: float32 [2, 768, 3, 768], P(None, ('dp', 'seq'), None, 'tensor')
- attention_output_weight_gradient: float32 [2, 768, 768], P(None, 'tensor', ('dp', 'seq'))
- ffn_input_weight_gradient: float32 [2, 768, 3072], P(None, ('dp', 'seq'), 'tensor')
- grad_w_back: float32 [2, 3072, 768], P(None, 'tensor', ('dp', 'seq'))
- grad_qv_bias: float32 [2, 2, 4, 192], P(None, None, 'tensor', ('dp', 'seq'))
- grad_mid_bias: float32 [2, 4, 768], P(None, 'tensor', ('dp', 'seq'))
- grad_shifts: float32 [2, 4, 768], P(None, None, ('dp', 'seq'))
- grad_gains: float32 [2, 2, 768], P(None, None, ('dp', 'seq'))
Inputs may be any that keep to these rules, and one draw needn't show every extreme that they name: `segment_ids`: ids never fall along a sequence, every id of the range occurs, and each sequence has one document of exactly 1600 tokens. `random_blocks`: for each sequence, head and query block the 3 blocks differ from one another, from the first and last block and from the query block and its two neighbours.
All inputs are finite; a program needn't handle non-finite values.
Results may differ from a plain program's by a relative error of at most 0.035.
Values may be sent and summed in bfloat16 or wider, within the bound.
A program may use at most 128 MiB of HBM per device.

v0:
```python
from functools import partial

import jax
import jax.numpy as jnp
from jax import lax
from jax.sharding import PartitionSpec as P

BLK = 64
LAYERS = 2
LENGTH = 2048


norm_eps = 1e-06


def normed(source, gain_row, shift_row):
    average = jnp.mean(source, axis=-1, keepdims=True)
    centered = source - average
    spread = jnp.mean(centered * centered, axis=-1, keepdims=True)
    return centered * lax.rsqrt(spread + norm_eps) * gain_row + shift_row


def position_lookup_matrix(query_block, random_rows, block_count):
    fixed_slots = jnp.stack(
        [
            query_block - 1,
            query_block,
            query_block + 1,
            jnp.zeros_like(query_block),
            jnp.zeros_like(query_block) + (block_count - 1),
        ],
        axis=1,
    )
    slot_live = jnp.stack(
        [
            query_block >= 1,
            query_block >= 0,
            query_block <= block_count - 2,
            query_block >= 2,
            query_block <= block_count - 3,
        ],
        axis=1,
    )
    fixed_slots = jnp.clip(fixed_slots, 0, block_count - 1)
    out_shape = random_rows.shape[:-1] + (5,)
    slot_index = jnp.concatenate([jnp.broadcast_to(fixed_slots, out_shape), random_rows], axis=-1)
    random_live = jnp.ones((slot_live.shape[0], random_rows.shape[-1]), dtype=jnp.bool_)
    return (slot_index, jnp.concatenate([slot_live, random_live], axis=1))


def fetch_layer(masters, layer_no):
    (
        query_key_value_weight,
        mixer_exit_projection_matrix,
        ffn_input_weight,
        perceptron_exit_matrix,
        qv_bias,
        mid_bias,
        shifts,
        gains,
    ) = [stacked[layer_no].astype(jnp.bfloat16) for stacked in masters]
    return (
        lax.all_gather(query_key_value_weight, ("dp", "seq"), axis=0, tiled=True),
        lax.all_gather(mixer_exit_projection_matrix, ("dp", "seq"), axis=1, tiled=True),
        lax.all_gather(ffn_input_weight, ("dp", "seq"), axis=0, tiled=True),
        lax.all_gather(perceptron_exit_matrix, ("dp", "seq"), axis=1, tiled=True),
        lax.all_gather(qv_bias, ("dp", "seq"), axis=2, tiled=True),
        lax.all_gather(mid_bias, ("dp", "seq"), axis=1, tiled=True),
        lax.all_gather(shifts, ("dp", "seq"), axis=1, tiled=True),
        lax.all_gather(gains, ("dp", "seq"), axis=1, tiled=True),
    )


def reduce_layer(gradients):
    g_qkv, g_out, g_in, g_back, g_qv, g_mid, g_shift, g_gain = gradients
    return (
        lax.psum_scatter(g_qkv, ("dp", "seq"), scatter_dimension=0, tiled=True),
        lax.psum_scatter(g_out, ("dp", "seq"), scatter_dimension=1, tiled=True),
        lax.psum_scatter(g_in, ("dp", "seq"), scatter_dimension=0, tiled=True),
        lax.psum_scatter(g_back, ("dp", "seq"), scatter_dimension=1, tiled=True),
        lax.psum_scatter(g_qv, ("dp", "seq"), scatter_dimension=2, tiled=True),
        lax.psum_scatter(g_mid, ("dp", "seq"), scatter_dimension=1, tiled=True),
        lax.psum_scatter(g_shift, ("dp", "seq"), scatter_dimension=1, tiled=True),
        lax.psum_scatter(g_gain, ("dp", "seq"), scatter_dimension=1, tiled=True),
    )


def residual_total(terms):
    return lax.psum(terms.astype(jnp.bfloat16), "tensor").astype(jnp.float32)


def input_grad_sum(terms):
    return lax.psum(terms.astype(jnp.bfloat16), "tensor").astype(jnp.float32)


def pick_blocks(gathered, flat_index, heads_local):
    seq_count, length_all, width_local = gathered.shape
    head_dim = width_local // heads_local
    block_count = length_all // BLK
    blocks = gathered.reshape(seq_count, block_count, BLK, heads_local, head_dim).transpose(
        0, 3, 1, 2, 4
    )
    offsets = (
        jnp.arange(seq_count, dtype=jnp.int32)[:, None] * heads_local
        + jnp.arange(heads_local, dtype=jnp.int32)[None, :]
    ) * block_count
    global_index = (flat_index + offsets[:, :, None]).reshape(-1)
    picked = jnp.take(
        blocks.reshape(seq_count * heads_local * block_count, BLK, head_dim), global_index, axis=0
    )
    return picked.reshape(seq_count, heads_local, flat_index.shape[2], BLK, head_dim)


def mixer_arguments(query_rows, key_all, value_all, segment, random_all, seq_index):
    seq_count, local_len, width_local = query_rows.shape
    heads_local = random_all.shape[1]
    head_dim = width_local // heads_local
    local_blocks = local_len // BLK
    block_count = LENGTH // BLK
    first_block = seq_index * local_blocks
    query_block = first_block + jnp.arange(local_blocks, dtype=jnp.int32)
    random_rows = lax.dynamic_slice_in_dim(random_all, first_block, local_blocks, axis=2)
    slot_index, slot_live = position_lookup_matrix(query_block, random_rows, block_count)
    slots = slot_index.shape[-1]
    flat_index = slot_index.reshape(seq_count, heads_local, -1)
    picked_keys = pick_blocks(key_all, flat_index, heads_local).reshape(
        seq_count, heads_local, local_blocks, slots * BLK, head_dim
    )
    picked_values = pick_blocks(value_all, flat_index, heads_local).reshape(
        seq_count, heads_local, local_blocks, slots * BLK, head_dim
    )
    seg_flat = segment.reshape(seq_count * block_count, BLK)
    seg_index = (
        flat_index + (jnp.arange(seq_count, dtype=jnp.int32) * block_count)[:, None, None]
    ).reshape(-1)
    key_segments = jnp.take(seg_flat, seg_index, axis=0).reshape(
        seq_count, heads_local, local_blocks, slots * BLK
    )
    query_segments = lax.dynamic_slice_in_dim(
        segment, seq_index * local_len, local_len, axis=1
    ).reshape(seq_count, 1, local_blocks, BLK)
    live_cols = jnp.repeat(slot_live, BLK, axis=1)
    allowed = live_cols[None, None, :, None, :] & (
        query_segments[..., None] == key_segments[:, :, :, None, :]
    )
    query_blocks = query_rows.reshape(
        seq_count, local_blocks, BLK, heads_local, head_dim
    ).transpose(0, 3, 1, 2, 4)
    scores = jnp.einsum(
        "shnad,shnkd->shnak", query_blocks, picked_keys, preferred_element_type=jnp.float32
    ) * head_dim ** (-0.5)
    masked = jnp.where(allowed, scores, -1e30)
    return (query_blocks, picked_keys, picked_values, flat_index, allowed, masked)


def softmax_total(allowed, masked):
    peak = jnp.max(masked, axis=-1, keepdims=True)
    expo = jnp.where(allowed, jnp.exp(masked - peak), 0.0)
    summed = jnp.sum(expo, axis=-1, keepdims=True)
    return (expo, summed, peak + jnp.log(summed))


def attend_forward(query_rows, key_all, value_all, segment, random_all, seq_index):
    query_blocks, picked_keys, picked_values, flat_index, allowed, masked = mixer_arguments(
        query_rows, key_all, value_all, segment, random_all, seq_index
    )
    expo, summed, logarithm_of_sum = softmax_total(allowed, masked)
    attn_probs = (expo / summed).astype(jnp.bfloat16)
    attention_result = jnp.einsum(
        "shnak,shnkd->shnad", attn_probs, picked_values, preferred_element_type=jnp.float32
    )
    seq_count, local_len, width_local = query_rows.shape
    attention_result = attention_result.transpose(0, 2, 3, 1, 4).reshape(
        seq_count, local_len, width_local
    )
    return (attention_result.astype(jnp.bfloat16), logarithm_of_sum)


def attend_backward(
    grad_mixed, query_rows, key_all, value_all, logarithm_of_sum, segment, random_all, seq_index
):
    query_blocks, picked_keys, picked_values, flat_index, allowed, masked = mixer_arguments(
        query_rows, key_all, value_all, segment, random_all, seq_index
    )
    attn_probs = jnp.where(allowed, jnp.exp(masked - logarithm_of_sum), 0.0)
    seq_count, heads_local, local_blocks, block_len, head_dim = query_blocks.shape
    grad_blocks = grad_mixed.reshape(
        seq_count, local_blocks, block_len, heads_local, head_dim
    ).transpose(0, 3, 1, 2, 4)
    grad_probs = jnp.einsum(
        "shnad,shnkd->shnak", grad_blocks, picked_values, preferred_element_type=jnp.float32
    )
    inner = jnp.sum(attn_probs * grad_probs, axis=-1, keepdims=True)
    grad_scores = (attn_probs * (grad_probs - inner)).astype(jnp.bfloat16)
    score_scale = head_dim ** (-0.5)
    grad_query = (
        jnp.einsum(
            "shnak,shnkd->shnad", grad_scores, picked_keys, preferred_element_type=jnp.float32
        )
        * score_scale
    )
    grad_keys = (
        jnp.einsum(
            "shnak,shnad->shnkd", grad_scores, query_blocks, preferred_element_type=jnp.float32
        )
        * score_scale
    )
    grad_values = jnp.einsum(
        "shnak,shnad->shnkd",
        attn_probs.astype(jnp.bfloat16),
        grad_blocks,
        preferred_element_type=jnp.float32,
    )
    block_count = LENGTH // BLK
    chooser = (flat_index[..., None] == jnp.arange(block_count, dtype=jnp.int32)).astype(
        jnp.float32
    )

    def spread_back(grad_picked):
        per_slot = grad_picked.reshape(seq_count, heads_local, -1, block_len, head_dim)
        placed = jnp.einsum("shjb,shjkd->shbkd", chooser, per_slot, precision=lax.Precision.HIGHEST)
        return placed.transpose(0, 2, 3, 1, 4).reshape(
            seq_count, block_count * block_len, heads_local * head_dim
        )

    grad_query = grad_query.transpose(0, 2, 3, 1, 4).reshape(
        seq_count, local_blocks * block_len, heads_local * head_dim
    )
    return (grad_query, spread_back(grad_keys), spread_back(grad_values))


def layer_forward(current, weights, segment, random_all, seq_index):
    (
        query_key_value_weight,
        mixer_exit_projection_matrix,
        ffn_input_weight,
        perceptron_exit_matrix,
        qv_bias,
        mid_bias,
        shifts,
        gains,
    ) = weights
    reduced_hidden_input = current.astype(jnp.bfloat16)
    query_key_value_full = jnp.einsum(
        "vmy,yhb->vmhb",
        reduced_hidden_input,
        query_key_value_weight,
        preferred_element_type=jnp.float32,
    )
    bias_rows = qv_bias.reshape(2, -1).astype(jnp.float32)
    query_rows = (query_key_value_full[:, :, 0] + bias_rows[0]).astype(jnp.bfloat16)
    key_rows = query_key_value_full[:, :, 1].astype(jnp.bfloat16)
    value_rows = (query_key_value_full[:, :, 2] + bias_rows[1]).astype(jnp.bfloat16)
    key_all, value_all = (
        lax.all_gather(key_rows, "seq", axis=1, tiled=True),
        lax.all_gather(value_rows, "seq", axis=1, tiled=True),
    )
    attention_result, logarithm_of_sum = attend_forward(
        query_rows, key_all, value_all, segment, random_all, seq_index
    )
    shift_all = shifts.astype(jnp.float32)
    gain_all = gains.astype(jnp.float32)
    before_first = (
        current
        + residual_total(
            jnp.einsum(
                "ruh,hn->run",
                attention_result,
                mixer_exit_projection_matrix,
                preferred_element_type=jnp.float32,
            )
        )
        + shift_all[0]
    )
    first = normed(before_first, gain_all[0], shift_all[1])
    reduced_leading = first.astype(jnp.bfloat16)
    pre_act = jnp.einsum(
        "jfw,wp->jfp", reduced_leading, ffn_input_weight, preferred_element_type=jnp.float32
    ) + mid_bias.reshape(-1).astype(jnp.float32)
    gelu_hidden = jax.nn.gelu(pre_act, approximate=True).astype(jnp.bfloat16)
    before_second = (
        first
        + residual_total(
            jnp.einsum(
                "yuv,vz->yuz",
                gelu_hidden,
                perceptron_exit_matrix,
                preferred_element_type=jnp.float32,
            )
        )
        + shift_all[2]
    )
    result = normed(before_second, gain_all[1], shift_all[3])
    stored = (
        reduced_hidden_input,
        query_rows,
        key_all,
        value_all,
        attention_result,
        logarithm_of_sum,
        before_first,
        reduced_leading,
        pre_act,
        gelu_hidden,
        before_second,
    )
    return (result, stored)


def layer_backward(grad_out, weights, stored, segment, random_all, seq_index):
    (
        query_key_value_weight,
        mixer_exit_projection_matrix,
        ffn_input_weight,
        perceptron_exit_matrix,
        qv_bias,
        mid_bias,
        shifts,
        gains,
    ) = weights
    (
        reduced_hidden_input,
        query_rows,
        key_all,
        value_all,
        attention_result,
        logarithm_of_sum,
        before_first,
        reduced_leading,
        pre_act,
        gelu_hidden,
        before_second,
    ) = stored
    shift_all = shifts.astype(jnp.float32)
    gain_all = gains.astype(jnp.float32)
    _, second_fn = jax.vjp(normed, before_second, gain_all[1], shift_all[3])
    grad_second, grad_gain2, grad_shift2 = second_fn(grad_out)
    grad_bias2 = jnp.sum(grad_second, axis=(0, 1))
    contracted_final_axis = grad_second.astype(jnp.bfloat16)
    grad_w_back = jnp.einsum(
        "yri,yrz->iz", gelu_hidden, contracted_final_axis, preferred_element_type=jnp.float32
    )
    gradient_gelu_hidden = jnp.einsum(
        "orm,gm->org",
        contracted_final_axis,
        perceptron_exit_matrix,
        preferred_element_type=jnp.float32,
    )
    _, gelu_fn = jax.vjp(partial(jax.nn.gelu, approximate=True), pre_act)
    gradient_preactivation = gelu_fn(gradient_gelu_hidden)[0].astype(jnp.bfloat16)
    grad_mid = jnp.sum(gradient_preactivation.astype(jnp.float32), axis=(0, 1))
    ffn_input_weight_gradient = jnp.einsum(
        "nfz,nfy->zy", reduced_leading, gradient_preactivation, preferred_element_type=jnp.float32
    )
    grad_first = grad_second + input_grad_sum(
        jnp.einsum(
            "yxm,rm->yxr",
            gradient_preactivation,
            ffn_input_weight,
            preferred_element_type=jnp.float32,
        )
    )
    _, first_fn = jax.vjp(normed, before_first, gain_all[0], shift_all[1])
    grad_before, grad_gain1, grad_shift1 = first_fn(grad_first)
    grad_bias_out = jnp.sum(grad_before, axis=(0, 1))
    reduced_prior = grad_before.astype(jnp.bfloat16)
    attention_output_weight_gradient = jnp.einsum(
        "xry,xru->yu", attention_result, reduced_prior, preferred_element_type=jnp.float32
    )
    grad_mixed = jnp.einsum(
        "avq,fq->avf",
        reduced_prior,
        mixer_exit_projection_matrix,
        preferred_element_type=jnp.float32,
    ).astype(jnp.bfloat16)
    grad_query, key_terms, value_terms = attend_backward(
        grad_mixed, query_rows, key_all, value_all, logarithm_of_sum, segment, random_all, seq_index
    )
    grad_keys, grad_values = (
        lax.psum_scatter(
            key_terms.astype(jnp.bfloat16), "seq", scatter_dimension=1, tiled=True
        ).astype(jnp.float32),
        lax.psum_scatter(
            value_terms.astype(jnp.bfloat16), "seq", scatter_dimension=1, tiled=True
        ).astype(jnp.float32),
    )
    layered_gradients = jnp.stack([grad_query, grad_keys, grad_values], axis=2).astype(jnp.bfloat16)
    derivative_joint_projection = jnp.einsum(
        "gth,gtmx->hmx", reduced_hidden_input, layered_gradients, preferred_element_type=jnp.float32
    )
    grad_qv = jnp.stack(
        [
            jnp.sum(layered_gradients[:, :, 0].astype(jnp.float32), axis=(0, 1)),
            jnp.sum(layered_gradients[:, :, 2].astype(jnp.float32), axis=(0, 1)),
        ]
    )
    grad_input = grad_before + input_grad_sum(
        jnp.einsum(
            "myib,qib->myq",
            layered_gradients,
            query_key_value_weight,
            preferred_element_type=jnp.float32,
        )
    )
    gradients = (
        derivative_joint_projection,
        attention_output_weight_gradient,
        ffn_input_weight_gradient,
        grad_w_back,
        grad_qv.reshape(2, 1, -1),
        grad_mid.reshape(1, -1),
        jnp.stack([grad_bias_out, grad_shift1, grad_bias2, grad_shift2]),
        jnp.stack([grad_gain1, grad_gain2]),
    )
    return (grad_input, gradients)


def shards(
    x_in,
    cotangent,
    segment_ids,
    random_blocks,
    query_key_value_weight,
    mixer_exit_projection_matrix,
    ffn_input_weight,
    perceptron_exit_matrix,
    qv_bias,
    mid_bias,
    shifts,
    gains,
):
    masters = (
        query_key_value_weight,
        mixer_exit_projection_matrix,
        ffn_input_weight,
        perceptron_exit_matrix,
        qv_bias,
        mid_bias,
        shifts,
        gains,
    )
    seq_index = lax.axis_index("seq")
    current = x_in.astype(jnp.float32)
    saved_weights = []
    saved_layers = []
    for layer_no in range(LAYERS):
        weights = fetch_layer(masters, layer_no)
        current, stored = layer_forward(current, weights, segment_ids, random_blocks, seq_index)
        saved_weights.append(weights)
        saved_layers.append(stored)
    gradient = cotangent.astype(jnp.float32)
    reduced = [None] * LAYERS
    for layer_no in range(LAYERS - 1, -1, -1):
        weights = fetch_layer(masters, layer_no)
        gradient, gradients = layer_backward(
            gradient, weights, saved_layers[layer_no], segment_ids, random_blocks, seq_index
        )
        reduced[layer_no] = reduce_layer(gradients)
    stacked_out = [
        jnp.stack([reduced[layer_no][member] for layer_no in range(LAYERS)]) for member in range(8)
    ]
    return (
        current.astype(jnp.bfloat16),
        gradient,
        stacked_out[0],
        stacked_out[1],
        stacked_out[2],
        stacked_out[3],
        stacked_out[4],
        stacked_out[5],
        stacked_out[6],
        stacked_out[7],
    )


def solution(mesh):
    in_specs = (
        P("dp", "seq", None),
        P("dp", "seq", None),
        P("dp", None),
        P("dp", "tensor", None, None),
        P(None, ("dp", "seq"), None, "tensor"),
        P(None, "tensor", ("dp", "seq")),
        P(None, ("dp", "seq"), "tensor"),
        P(None, "tensor", ("dp", "seq")),
        P(None, None, "tensor", ("dp", "seq")),
        P(None, "tensor", ("dp", "seq")),
        P(None, None, ("dp", "seq")),
        P(None, None, ("dp", "seq")),
    )
    out_specs = (
        P("dp", "seq", None),
        P("dp", "seq", None),
        P(None, ("dp", "seq"), None, "tensor"),
        P(None, "tensor", ("dp", "seq")),
        P(None, ("dp", "seq"), "tensor"),
        P(None, "tensor", ("dp", "seq")),
        P(None, None, "tensor", ("dp", "seq")),
        P(None, "tensor", ("dp", "seq")),
        P(None, None, ("dp", "seq")),
        P(None, None, ("dp", "seq")),
    )
    return jax.shard_map(shards, mesh=mesh, in_specs=in_specs, out_specs=out_specs, check_vma=False)
```

profile of v0, /device:TPU:0, one launch (start us, length us, event | category | flops | bytes accessed | tf_op | source)
XLA Modules:
  0.0 1928.2 jit_solution(15131960421746591890)
XLA Ops:
  10.4 41.6 %all-gather = bf16[1,768,3,192]{3,2,0,1:T(4,128)(2,1)S(1)} all-gather(bf16[1,96,3,192]{3,2,0,1:T(4,128)(2,1)S(1)} %get-tuple-element.106), channel_id=2, replica_groups=mesh['dp'=2,'seq'=4,'tensor'=4] {'dp','seq'}, dimensions={1}, use_global_device_ids=true | all-gather | bytes 995328 | tf_op jit(solution)/shard_map/all_gather | solution.py:63
  59.0 30.7 %all-gather.1 = bf16[1,2,1,192]{2,1,0,3:T(2,128)(2,1)S(1)} all-gather(bf16[1,2,1,24]{2,1,0,3:T(2,128)(2,1)S(1)} %get-tuple-element.119), channel_id=3, replica_groups=mesh['dp'=2,'seq'=4,'tensor'=4] {'dp','seq'}, dimensions={3}, use_global_device_ids=true | all-gather | bytes 864 | tf_op jit(solution)/shard_map/all_gather | solution.py:67
  91.9 34.0 %all-gather.3 = bf16[1,192,768]{1,0,2:T(2,128)(2,1)S(1)} all-gather(bf16[1,192,96]{1,0,2:T(2,128)(2,1)S(1)} %get-tuple-element.113), channel_id=5, replica_groups=mesh['dp'=2,'seq'=4,'tensor'=4] {'dp','seq'}, dimensions={2}, use_global_device_ids=true | all-gather | bytes 331776 | tf_op jit(solution)/shard_map/all_gather | solution.py:64
  127.5 18.3 all-gather.2
  145.8 15.7 all_gather.73
  197.0 20.6 %all-reduce.5 = (bf16[768]{0:T(1024)(128)(2,1)}, bf16[768]{0:T(1024)(128)(2,1)S(1)}) all-reduce(bf16[768]{0:T(1024)(128)(2,1)S(1)} %dynamic-update-slice.1, bf16[768]{0:T(1024)(128)(2,1)S(1)} %dynamic-update-slice), channel_id=18, replica_groups=mesh['dp'=2,'seq'=4,'tensor'=4] {'dp','seq'}, use_global_device_ids=true, to_apply=%add.1 | all-reduce | flops 1536 | bytes 6144
  221.4 31.1 %all-gather.10 = bf16[1,2,1,192]{2,1,0,3:T(2,128)(2,1)S(1)} all-gather(bf16[1,2,1,24]{2,1,0,3:T(2,128)(2,1)} %get-tuple-element.118), channel_id=12, replica_groups=mesh['dp'=2,'seq'=4,'tensor'=4] {'dp','seq'}, dimensions={3}, use_global_device_ids=true | all-gather | bytes 864 | tf_op jit(solution)/shard_map/all_gather | solution.py:67
  252.6 32.2 %all-gather.4 = bf16[1,4,768]{1,0,2:T(2,128)(2,1)S(1)} all-gather(bf16[1,4,96]{1,0,2:T(2,128)(2,1)S(1)} %get-tuple-element.116), channel_id=6, replica_groups=mesh['dp'=2,'seq'=4,'tensor'=4] {'dp','seq'}, dimensions={2}, use_global_device_ids=true | all-gather | bytes 6912 | tf_op jit(solution)/shard_map/all_gather | solution.py:69
  285.9 31.7 %all-gather.5 = bf16[1,2,768]{1,0,2:T(2,128)(2,1)S(1)} all-gather(bf16[1,2,96]{1,0,2:T(2,128)(2,1)S(1)} %get-tuple-element.115), channel_id=7, replica_groups=mesh['dp'=2,'seq'=4,'tensor'=4] {'dp','seq'}, dimensions={2}, use_global_device_ids=true | all-gather | bytes 3456 | tf_op jit(solution)/shard_map/all_gather | solution.py:70
  319.2 4.6 slice_reduce_fusion.7
  323.8 11.2 slice_reduce_fusion.6
  338.0 4.0 convolution_add_fusion.1
  345.8 36.3 %all-gather.12 = bf16[1,192,768]{1,0,2:T(2,128)(2,1)} all-gather(bf16[1,192,96]{1,0,2:T(2,128)(2,1)} %get-tuple-element.112), channel_id=14, replica_groups=mesh['dp'=2,'seq'=4,'tensor'=4] {'dp','seq'}, dimensions={2}, use_global_device_ids=true | all-gather | bytes 331776 | tf_op jit(solution)/shard_map/all_gather | solution.py:64
  385.0 39.0 %all-gather.9 = bf16[1,768,3,192]{3,2,0,1:T(4,128)(2,1)} all-gather(bf16[1,96,3,192]{3,2,0,1:T(4,128)(2,1)} %get-tuple-element.107), channel_id=11, replica_groups=mesh['dp'=2,'seq'=4,'tensor'=4] {'dp','seq'}, dimensions={1}, use_global_device_ids=true | all-gather | bytes 995328 | tf_op jit(solution)/shard_map/all_gather | solution.py:63
  436.9 16.6 all-gather.11
  453.4 16.7 all_gather.83
  483.4 4.1 gather_fusion.3
  487.5 4.1 gather_fusion.4
  509.8 32.4 %all-gather.14 = bf16[1,2,768]{1,0,2:T(2,128)(2,1)S(1)} all-gather(bf16[1,2,96]{1,0,2:T(2,128)(2,1)} %get-tuple-element.114), channel_id=16, replica_groups=mesh['dp'=2,'seq'=4,'tensor'=4] {'dp','seq'}, dimensions={2}, use_global_device_ids=true | all-gather | bytes 3456 | tf_op jit(solution)/shard_map/all_gather | solution.py:70
  542.6 32.3 %all-gather.13 = bf16[1,4,768]{1,0,2:T(2,128)(2,1)S(1)} all-gather(bf16[1,4,96]{1,0,2:T(2,128)(2,1)S(1)} %copy-done.52), channel_id=15, replica_groups=mesh['dp'=2,'seq'=4,'tensor'=4] {'dp','seq'}, dimensions={2}, use_global_device_ids=true | all-gather | bytes 6912 | tf_op jit(solution)/shard_map/all_gather | solution.py:69
  575.3 4.6 slice_reduce_fusion.1
  579.9 11.2 slice_reduce_fusion
  595.1 3.8 convolution_add_fusion
  602.7 35.4 %all-reduce.21.cloned.1.call-done = bf16[1,512,768]{2,1,0:T(8,128)(2,1)} async-done(((bf16[1,512,768]{2,1,0:T(8,128)(2,1)}), bf16[1,512,768]{2,1,0:T(8,128)(2,1)}) %all-reduce.21.cloned.1.call-update) | async-done | bytes 786448 | tf_op jit(solution)/shard_map/psum | solution.py:89
  650.5 34.0 %all-reduce.23.cloned.1.call-done = bf16[1,512,768]{2,1,0:T(8,128)(2,1)} async-done(((bf16[1,512,768]{2,1,0:T(8,128)(2,1)}), bf16[1,512,768]{2,1,0:T(8,128)(2,1)}) %all-reduce.23.cloned.1.call-update) | async-done | bytes 786448 | tf_op jit(solution)/shard_map/psum | solution.py:93
  684.4 3.7 multiply_reduce_fusion.2
  693.3 4.7 multiply_reduce_fusion.1
  705.0 5.6 reshape.1352
  710.6 7.7 copy.168
  718.2 6.4 fusion.28
  724.6 4.1 copy.169
  739.1 6.0 reshape.1353
  745.1 7.7 copy.171
  752.8 6.4 fusion.29
  759.3 4.2 copy.172
  767.1 4.4 convert_reduce_fusion.3
  775.4 15.1 reduce-scatter.43.cloned.1.call-done
  793.8 34.0 %all-reduce.25.cloned.1.call-done = bf16[1,512,768]{2,1,0:T(8,128)(2,1)} async-done(((bf16[1,512,768]{2,1,0:T(8,128)(2,1)}), bf16[1,512,768]{2,1,0:T(8,128)(2,1)}) %all-reduce.25.cloned.1.call-update) | async-done | bytes 786448 | tf_op jit(solution)/shard_map/psum | solution.py:93
  827.8 3.7 multiply_reduce_fusion.3
  838.9 34.1 %all-reduce.27.cloned.1.call-done = bf16[1,512,768]{2,1,0:T(8,128)(2,1)} async-done(((bf16[1,512,768]{2,1,0:T(8,128)(2,1)}), bf16[1,512,768]{2,1,0:T(8,128)(2,1)}) %all-reduce.27.cloned.1.call-update) | async-done | bytes 786448 | tf_op jit(solution)/shard_map/psum | solution.py:93
  873.0 3.9 multiply_reduce_fusion.4
  892.7 5.6 reshape.1358
  898.3 7.7 copy.179
  906.0 6.4 fusion.30
  912.4 4.1 copy.180
  927.9 7.7 copy.182
  935.6 5.3 fusion.31
  951.0 20.2 %reduce-scatter.47.cloned.1.call-done = bf16[1,512,192]{1,2,0:T(8,128)(2,1)} async-done(((bf16[1,2048,192]{1,2,0:T(8,128)(2,1)}), bf16[1,512,192]{1,2,0:T(8,128)(2,1)}) %reduce-scatter.47.cloned.1.call-update) | async-done | bytes 196624 | tf_op jit(solution)/shard_map/reduce_scatter | solution.py:383
  983.2 25.5 %all-reduce.29.cloned.1.call-done = bf16[1,512,768]{2,1,0:T(8,128)(2,1)} async-done(((bf16[1,512,768]{2,1,0:T(8,128)(2,1)}), bf16[1,512,768]{2,1,0:T(8,128)(2,1)}) %all-reduce.29.cloned.1.call-update) | async-done | bytes 786448 | tf_op jit(solution)/shard_map/psum | solution.py:93
  1017.4 4.0 fusion.142
  1040.9 62.9 %reduce-scatter.75.cloned.1.call-done = f32[96,2]{1,0:T(8,128)} async-done(((f32[768,2]{1,0:T(8,128)}), f32[96,2]{1,0:T(8,128)}) %reduce-scatter.75.cloned.1.call-update) | async-done | bytes 784
  1104.7 64.0 %reduce-scatter.63.cloned.1.call-done = f32[96,192]{1,0:T(8,128)} async-done(((f32[768,192]{1,0:T(8,128)}), f32[96,192]{1,0:T(8,128)}) %reduce-scatter.63.cloned.1.call-update) | async-done | bytes 73744
  1169.8 63.5 %reduce-scatter.65.cloned.1.call-done = f32[96,1]{1,0:T(8,128)} async-done(((f32[768,1]{1,0:T(8,128)}), f32[96,1]{1,0:T(8,128)}) %reduce-scatter.65.cloned.1.call-update) | async-done | bytes 400
  1234.7 63.2 %reduce-scatter.71.cloned.1.call-done = f32[96,4]{1,0:T(8,128)} async-done(((f32[768,4]{1,0:T(8,128)}), f32[96,4]{1,0:T(8,128)}) %reduce-scatter.71.cloned.1.call-update) | async-done | bytes 1552
  1298.8 63.2 %reduce-scatter.73.cloned.1.call-done = f32[96,2]{1,0:T(8,128)} async-done(((f32[768,2]{1,0:T(8,128)}), f32[96,2]{1,0:T(8,128)}) %reduce-scatter.73.cloned.1.call-update) | async-done | bytes 784
  1363.5 63.7 %reduce-scatter.61.cloned.1.call-done = f32[96,192]{1,0:T(8,128)} async-done(((f32[768,192]{1,0:T(8,128)}), f32[96,192]{1,0:T(8,128)}) %reduce-scatter.61.cloned.1.call-update) | async-done | bytes 73744
  1429.0 19.5 %all-reduce.4 = (f32[2,1,192]{2,0,1:T(2,128)S(1)}, f32[2,1,192]{2,0,1:T(2,128)S(1)}) all-reduce(f32[2,1,192]{2,0,1:T(2,128)S(1)} %maximum_bitcast_fusion.1, f32[2,1,192]{2,0,1:T(2,128)S(1)} %maximum_bitcast_fusion), channel_id=33, replica_groups=mesh['dp'=2,'seq'=4,'tensor'=4] {'dp','seq'}, use_global_device_ids=true, to_apply=%region_47.50.clone | all-reduce | flops 768 | bytes 6144
  1449.2 41.9 %reduce-scatter.69.cloned.1.call-done = f32[96,4]{1,0:T(8,128)} async-done(((f32[768,4]{1,0:T(8,128)}), f32[96,4]{1,0:T(8,128)}) %reduce-scatter.69.cloned.1.call-update) | async-done | bytes 1552
  1492.6 67.9 %reduce-scatter.59.cloned.1.call-done = f32[96,576]{1,0:T(8,128)} async-done(((f32[768,576]{1,0:T(8,128)}), f32[96,576]{1,0:T(8,128)}) %reduce-scatter.59.cloned.1.call-update) | async-done | bytes 221200
  1561.6 70.9 %reduce-scatter.55.cloned.1.call-done = f32[768,96]{0,1:T(8,128)} async-done(((f32[768,768]{0,1:T(8,128)}), f32[768,96]{0,1:T(8,128)}) %reduce-scatter.55.cloned.1.call-update) | async-done | bytes 294928 | tf_op jit(solution)/shard_map/reduce_scatter | solution.py:80
  1632.4 72.0 %reduce-scatter.53.cloned.1.call-done = f32[768,96]{0,1:T(8,128)} async-done(((f32[768,768]{0,1:T(8,128)}), f32[768,96]{0,1:T(8,128)}) %reduce-scatter.53.cloned.1.call-update) | async-done | bytes 294928 | tf_op jit(solution)/shard_map/reduce_scatter | solution.py:80
  1706.3 70.2 %reduce-scatter.51.cloned.1.call-done = f32[96,768]{1,0:T(8,128)} async-done(((f32[768,768]{1,0:T(8,128)}), f32[96,768]{1,0:T(8,128)}) %reduce-scatter.51.cloned.1.call-update) | async-done | bytes 294928 | tf_op jit(solution)/shard_map/reduce_scatter | solution.py:79
  1776.5 72.0 %reduce-scatter.49.cloned.1.call-done = f32[96,768]{1,0:T(8,128)} async-done(((f32[768,768]{1,0:T(8,128)}), f32[96,768]{1,0:T(8,128)}) %reduce-scatter.49.cloned.1.call-update) | async-done | bytes 294928 | tf_op jit(solution)/shard_map/reduce_scatter | solution.py:79
  1850.5 67.8 %reduce-scatter.57.cloned.1.call-done = f32[96,576]{1,0:T(8,128)} async-done(((f32[768,576]{1,0:T(8,128)}), f32[96,576]{1,0:T(8,128)}) %reduce-scatter.57.cloned.1.call-update) | async-done | bytes 221200
  (583 shorter events, 261.5 us)
Async XLA Ops:
  8.0 47.1 %copy-start = (s32[1,3,32,3]{2,0,3,1:T(1,128)S(1)}, s32[1,3,32,3]{2,0,3,1:T(1,128)}, u32[]{:S(2)}) copy-start(s32[1,3,32,3]{2,0,3,1:T(1,128)} %param.19) | copy-start | bytes 3460
  8.0 327.0 %all-reduce.15.cloned.1.call-start = ((), (), s32[]{:S(2)}) async-start(), calls=%async_computation.18 | async-start | bytes 1572864 | tf_op jit(solution)/shard_map/psum | solution.py:89
  54.5 36.4 %copy-start.49 = (f32[2,192,96]{2,1,0:T(8,128)S(1)}, f32[2,192,96]{2,1,0:T(8,128)}, u32[]{:S(2)}) copy-start(f32[2,192,96]{2,1,0:T(8,128)} %param.21) | copy-start | bytes 442372
  56.8 119.2 %copy-start.121 = (pred[192]{0:T(512)(128)(4,1)}, pred[192]{0:T(512)(128)(4,1)S(1)}, u32[]{:S(2)}) copy-start(pred[192]{0:T(512)(128)(4,1)S(1)} %get-tuple-element.101) | copy-start | bytes 580
  57.3 116.0 %copy-start.116 = (s32[1024]{0:T(1024)}, s32[1024]{0:T(1024)S(1)}, u32[]{:S(2)}) copy-start(s32[1024]{0:T(1024)S(1)} %pad_clamp_fusion) | copy-start | bytes 12292
  90.9 88.5 %copy-start.84 = (f32[3,64]{1,0:T(4,128)}, f32[3,64]{1,0:T(4,128)S(1)}, u32[]{:S(2)}) copy-start(f32[3,64]{1,0:T(4,128)S(1)} %add.476) | copy-start | bytes 2308
  191.4 26.9 %copy-start.127 = (f32[2,4,96]{2,1,0:T(4,128)S(1)}, f32[2,4,96]{2,1,0:T(4,128)}, u32[]{:S(2)}) copy-start(f32[2,4,96]{2,1,0:T(4,128)} %param.26) | copy-start | bytes 9220
  191.4 146.6 %all-gather.23.cloned.1.call-start = ((), (), s32[]{:S(2)}) async-start(), calls=%async_computation.34 | async-start | bytes 1327104 | tf_op jit(solution)/shard_map/all_gather | solution.py:65
  193.3 148.7 %all-gather.25.cloned.1.call-start = ((), (), s32[]{:S(2)}) async-start(), calls=%async_computation.35 | async-start | bytes 1327104 | tf_op jit(solution)/shard_map/all_gather | solution.py:66
  195.2 232.2 %all-reduce.17.cloned.1.call-start = ((), (), s32[]{:S(2)}) async-start(), calls=%async_computation.19 | async-start | bytes 1572864 | tf_op jit(solution)/shard_map/psum | solution.py:89
  323.8 106.4 %copy-start.61 = (f32[768]{0:T(1024)}, f32[768]{0:T(1024)S(1)}, u32[]{:S(2)}) copy-start(f32[768]{0:T(1024)S(1)} %get-tuple-element.73) | copy-start | bytes 9220
  335.0 92.4 %copy-start.108 = (f32[768]{0:T(1024)}, f32[768]{0:T(1024)S(1)}, u32[]{:S(2)}) copy-start(f32[768]{0:T(1024)S(1)} %get-tuple-element.77) | copy-start | bytes 9220
  335.0 95.2 %copy-start.99 = (f32[768]{0:T(1024)}, f32[768]{0:T(1024)S(1)}, u32[]{:S(2)}) copy-start(f32[768]{0:T(1024)S(1)} %get-tuple-element.75) | copy-start | bytes 9220
  336.9 90.5 %copy-start.63 = (f32[512]{0:T(512)}, f32[512]{0:T(512)S(1)}, u32[]{:S(2)}) copy-start(f32[512]{0:T(512)S(1)} %broadcast_multiply_fusion.3) | copy-start | bytes 6148
  338.0 89.4 %copy-start.74 = (f32[512]{0:T(512)}, f32[512]{0:T(512)S(1)}, u32[]{:S(2)}) copy-start(f32[512]{0:T(512)S(1)} %fusion.123) | copy-start | bytes 6148
  345.7 245.4 %all-reduce.19.cloned.1.call-start = ((), (), s32[]{:S(2)}) async-start(), calls=%async_computation.20 | async-start | bytes 1572864 | tf_op jit(solution)/shard_map/psum | solution.py:89
  382.1 113.0 %copy-start.88 = (f32[3,64]{1,0:T(4,128)}, f32[3,64]{1,0:T(4,128)S(1)}, u32[]{:S(2)}) copy-start(f32[3,64]{1,0:T(4,128)S(1)} %add.505) | copy-start | bytes 2308
  504.8 37.8 %copy-start.52 = (bf16[1,4,96]{1,0,2:T(2,128)(2,1)S(1)}, bf16[1,4,96]{1,0,2:T(2,128)(2,1)}, u32[]{:S(2)}) copy-start(bf16[1,4,96]{1,0,2:T(2,128)(2,1)} %get-tuple-element.117) | copy-start | bytes 2308
  507.2 87.9 %all-gather.27.cloned.1.call-start = ((), (), s32[]{:S(2)}) async-start(), calls=%async_computation.36 | async-start | bytes 1327104 | tf_op jit(solution)/shard_map/all_gather | solution.py:65
  507.7 91.2 %all-gather.29.cloned.1.call-start = ((), (), s32[]{:S(2)}) async-start(), calls=%async_computation.37 | async-start | bytes 1327104 | tf_op jit(solution)/shard_map/all_gather | solution.py:66
  508.5 129.7 %all-reduce.21.cloned.1.call-start = ((), (), s32[]{:S(2)}) async-start(), calls=%async_computation.21 | async-start | bytes 1572864 | tf_op jit(solution)/shard_map/psum | solution.py:89
  574.9 16.3 copy-start.62
  574.9 16.3 copy-start.67
  574.9 16.3 copy-start.78
  574.9 16.3 copy-start.100
  591.1 47.0 %copy-start.101 = (f32[768]{0:T(1024)}, f32[768]{0:T(1024)S(1)}, u32[]{:S(2)}) copy-start(f32[768]{0:T(1024)S(1)} %get-tuple-element.71) | copy-start | bytes 9220
  593.5 94.7 %copy-start.68 = (f32[512]{0:T(512)}, f32[512]{0:T(512)S(1)}, u32[]{:S(2)}) copy-start(f32[512]{0:T(512)S(1)} %broadcast_multiply_fusion.1) | copy-start | bytes 6148
  595.0 43.1 %copy-start.79 = (f32[512]{0:T(512)}, f32[512]{0:T(512)S(1)}, u32[]{:S(2)}) copy-start(f32[512]{0:T(512)S(1)} %fusion.125) | copy-start | bytes 6148
  602.6 81.8 %all-reduce.23.cloned.1.call-start = ((), (), s32[]{:S(2)}) async-start(), calls=%async_computation.22 | async-start | bytes 1572864 | tf_op jit(solution)/shard_map/psum | solution.py:93
  649.6 125.8 %reduce-scatter.41.cloned.1.call-start = ((), (), s32[]{:S(2)}) async-start(), calls=%async_computation.23 | async-start | bytes 983040 | tf_op jit(solution)/shard_map/reduce_scatter | solution.py:380
  650.4 37.7 %copy-start.98 = (f32[512]{0:T(512)S(1)}, f32[512]{0:T(512)}, u32[]{:S(2)}) copy-start(f32[512]{0:T(512)} %copy-done.97) | copy-start | bytes 6148
  650.4 37.7 %copy-start.80 = (f32[512]{0:T(512)S(1)}, f32[512]{0:T(512)}, u32[]{:S(2)}) copy-start(f32[512]{0:T(512)} %copy-done.79) | copy-start | bytes 6148
  650.4 37.7 %copy-start.91 = (f32[512]{0:T(512)S(1)}, f32[512]{0:T(512)}, u32[]{:S(2)}) copy-start(f32[512]{0:T(512)} %copy-done.90) | copy-start | bytes 6148
  689.1 142.5 %copy-start.70 = (f32[512]{0:T(512)}, f32[512]{0:T(512)S(1)}, u32[]{:S(2)}) copy-start(f32[512]{0:T(512)S(1)} %negate_multiply_fusion.2) | copy-start | bytes 6148
  732.3 58.2 %reduce-scatter.43.cloned.1.call-start = ((), (), s32[]{:S(2)}) async-start(), calls=%async_computation.24 | async-start | bytes 983040 | tf_op jit(solution)/shard_map/reduce_scatter | solution.py:383
  767.0 60.8 %all-reduce.25.cloned.1.call-start = ((), (), s32[]{:S(2)}) async-start(), calls=%async_computation.25 | async-start | bytes 1572864 | tf_op jit(solution)/shard_map/psum | solution.py:93
  793.7 37.8 %copy-start.96 = (f32[512]{0:T(512)S(1)}, f32[512]{0:T(512)}, u32[]{:S(2)}) copy-start(f32[512]{0:T(512)} %copy-done.95) | copy-start | bytes 6148
  793.7 79.2 %all-reduce.27.cloned.1.call-start = ((), (), s32[]{:S(2)}) async-start(), calls=%async_computation.26 | async-start | bytes 1572864 | tf_op jit(solution)/shard_map/psum | solution.py:93
  832.4 44.4 %copy-start.86 = (f32[512]{0:T(512)}, f32[512]{0:T(512)S(1)}, u32[]{:S(2)}) copy-start(f32[512]{0:T(512)S(1)} %negate_multiply_fusion.1) | copy-start | bytes 6148
  836.4 36.6 %copy-start.64 = (f32[512]{0:T(512)S(1)}, f32[512]{0:T(512)}, u32[]{:S(2)}) copy-start(f32[512]{0:T(512)} %copy-done.63) | copy-start | bytes 6148
  836.4 36.6 %copy-start.75 = (f32[512]{0:T(512)S(1)}, f32[512]{0:T(512)}, u32[]{:S(2)}) copy-start(f32[512]{0:T(512)} %copy-done.74) | copy-start | bytes 6148
  838.1 112.9 %reduce-scatter.45.cloned.1.call-start = ((), (), s32[]{:S(2)}) async-start(), calls=%async_computation.27 | async-start | bytes 983040 | tf_op jit(solution)/shard_map/reduce_scatter | solution.py:380
  838.9 38.0 %copy-start.94 = (f32[512]{0:T(512)S(1)}, f32[512]{0:T(512)}, u32[]{:S(2)}) copy-start(f32[512]{0:T(512)} %copy-done.93) | copy-start | bytes 6148
  920.1 51.1 %reduce-scatter.47.cloned.1.call-start = ((), (), s32[]{:S(2)}) async-start(), calls=%async_computation.28 | async-start | bytes 983040 | tf_op jit(solution)/shard_map/reduce_scatter | solution.py:383
  947.7 61.0 %all-reduce.29.cloned.1.call-start = ((), (), s32[]{:S(2)}) async-start(), calls=%async_computation.29 | async-start | bytes 1572864 | tf_op jit(solution)/shard_map/psum | solution.py:93
  951.0 20.3 %copy-start.53 = (bf16[512,1,192]{0,2,1:T(8,128)(2,1)}, bf16[512,1,192]{0,2,1:T(8,128)(2,1)S(1)}, u32[]{:S(2)}) copy-start(bf16[512,1,192]{0,2,1:T(8,128)(2,1)S(1)} %stack.211) | copy-start | bytes 589828
  974.4 65.5 %reduce-scatter.67.cloned.1.call-start = ((), (), s32[]{:S(2)}) async-start(), calls=%async_computation.43 | async-start | bytes 442368
  975.5 128.3 %reduce-scatter.75.cloned.1.call-start = ((), (), s32[]{:S(2)}) async-start(), calls=%async_computation.47 | async-start | bytes 442368
  976.6 192.0 %reduce-scatter.63.cloned.1.call-start = ((), (), s32[]{:S(2)}) async-start(), calls=%async_computation.41 | async-start | bytes 884736
  978.2 255.0 %reduce-scatter.65.cloned.1.call-start = ((), (), s32[]{:S(2)}) async-start(), calls=%async_computation.42 | async-start | bytes 442368
  979.3 318.6 %reduce-scatter.71.cloned.1.call-start = ((), (), s32[]{:S(2)}) async-start(), calls=%async_computation.45 | async-start | bytes 442368
  980.3 381.7 %reduce-scatter.73.cloned.1.call-start = ((), (), s32[]{:S(2)}) async-start(), calls=%async_computation.46 | async-start | bytes 442368
  981.4 445.7 %reduce-scatter.61.cloned.1.call-start = ((), (), s32[]{:S(2)}) async-start(), calls=%async_computation.40 | async-start | bytes 884736
  983.0 508.1 %reduce-scatter.69.cloned.1.call-start = ((), (), s32[]{:S(2)}) async-start(), calls=%async_computation.44 | async-start | bytes 442368
  983.2 29.2 %copy-start.6 = (f32[1,512,768]{2,1,0:T(8,128)S(1)}, f32[1,512,768]{2,1,0:T(8,128)}, u32[]{:S(2)}) copy-start(f32[1,512,768]{2,1,0:T(8,128)} %copy-done.4) | copy-start | bytes 4718596
  983.2 29.2 %copy-start.50 = (bf16[1,512,192]{1,2,0:T(8,128)(2,1)S(1)}, bf16[1,512,192]{1,2,0:T(8,128)(2,1)}, u32[]{:S(2)}) copy-start(bf16[1,512,192]{1,2,0:T(8,128)(2,1)} %reduce-scatter.43.cloned.1.call-done) | copy-start | bytes 589828
  1012.3 548.2 %reduce-scatter.59.cloned.1.call-start = ((), (), s32[]{:S(2)}) async-start(), calls=%async_computation.39 | async-start | bytes 2211840
  1016.0 616.4 %reduce-scatter.55.cloned.1.call-start = ((), (), s32[]{:S(2)}) async-start(), calls=%async_computation.33 | async-start | bytes 2654208 | tf_op jit(solution)/shard_map/reduce_scatter | solution.py:80
  1021.4 683.0 %reduce-scatter.53.cloned.1.call-start = ((), (), s32[]{:S(2)}) async-start(), calls=%async_computation.32 | async-start | bytes 2654208 | tf_op jit(solution)/shard_map/reduce_scatter | solution.py:80
  1025.3 751.2 %reduce-scatter.51.cloned.1.call-start = ((), (), s32[]{:S(2)}) async-start(), calls=%async_computation.31 | async-start | bytes 2654208 | tf_op jit(solution)/shard_map/reduce_scatter | solution.py:79
  1030.5 818.1 %reduce-scatter.49.cloned.1.call-start = ((), (), s32[]{:S(2)}) async-start(), calls=%async_computation.30 | async-start | bytes 2654208 | tf_op jit(solution)/shard_map/reduce_scatter | solution.py:79
  1034.4 883.9 %reduce-scatter.57.cloned.1.call-start = ((), (), s32[]{:S(2)}) async-start(), calls=%async_computation.38 | async-start | bytes 2211840
  1037.9 260.8 %copy-start.120 = (f32[3,64]{1,0:T(4,128)S(1)}, f32[3,64]{1,0:T(4,128)}, u32[]{:S(2)}) copy-start(f32[3,64]{1,0:T(4,128)} %get-tuple-element.139) | copy-start | bytes 2308
  1848.5 72.0 %copy-start.1 = (s32[1,3,32,3]{2,0,3,1:T(1,128)S(1)}, s32[1,3,32,3]{2,0,3,1:T(1,128)}, u32[]{:S(2)}) copy-start(s32[1,3,32,3]{2,0,3,1:T(1,128)} %param.19) | copy-start | bytes 3460
  (108 other events, 254.1 us)
Sparse Core Ops, SparseCore 0:
  191.5 34.2 all-reduce.14
  345.9 33.2 all-reduce.16
  507.3 35.5 all-reduce.18
  602.8 35.3 all-reduce.20
  649.7 34.6 all-reduce.22
  732.5 23.3 reduce-scatter.40
  767.1 23.3 reduce-scatter.42
  793.8 33.8 all-reduce.24
  838.3 34.6 all-reduce.26
  920.3 23.3 reduce-scatter.44
  947.8 23.3 reduce-scatter.46
  974.6 34.0 all-reduce.28
Sparse Core Ops, SparseCore 1:
  194.6 41.2 all-gather.22
  238.4 41.1 all-gather.24
  509.7 42.6 all-gather.26
  554.5 40.3 all-gather.28
  979.1 60.8 reduce-scatter.66
  1043.2 60.5 reduce-scatter.74
  1107.0 61.6 reduce-scatter.62
  1172.7 60.5 reduce-scatter.64
  1237.3 60.5 reduce-scatter.70
  1301.5 60.5 reduce-scatter.72
  1365.5 61.6 reduce-scatter.60
  1430.5 60.6 reduce-scatter.68
  1494.4 66.0 reduce-scatter.58
  1564.4 68.0 reduce-scatter.54
  1636.3 68.0 reduce-scatter.52
  1708.3 68.1 reduce-scatter.50
  1780.4 68.1 reduce-scatter.48
  1852.4 65.8 reduce-scatter.56
where the time goes:
time: 1940 us; the launch traced here: 1930 us
  waiting for transfers between devices  1040 us (54%)
  blocking collectives  449 us (23%)
  local copies, waits for them, and re-layouts  246 us (13%)
  matrix products  110 us (6%)
  other arithmetic  58.4 us (3%)
    unnamed x40, waiting for transfers between devices  561 us
    reduce_scatter x2, waiting for transfers between devices, reduce_layer(): lax.psum_scatter(g_back, ('dp', 'seq'), scatter_dimension=1, tiled=True)  143 us
    reduce_scatter x2, waiting for transfers between devices, reduce_layer(): lax.psum_scatter(g_in, ('dp', 'seq'), scatter_dimension=0, tiled=True)  142 us
    psum x4, waiting for transfers between devices, input_grad_sum(): return lax.psum(terms.astype(jnp.bfloat16), 'tensor').astype(jnp.float32)  128 us
    all_gather x2, blocking collectives, fetch_layer(): lax.all_gather(query_key_value_weight, ('dp', 'seq'), axis=0, tiled=True)  80.6 us
    all_gather x2, blocking collectives, fetch_layer(): lax.all_gather(mixer_exit_projection_matrix, ('dp', 'seq'), axis=1, tiled...  70.3 us
    all_gather x2, blocking collectives, fetch_layer(): lax.all_gather(shifts, ('dp', 'seq'), axis=1, tiled=True)  64.5 us
    all_gather x2, blocking collectives, fetch_layer(): lax.all_gather(gains, ('dp', 'seq'), axis=1, tiled=True)  64.1 us
  transfers between devices with their start and end apart: 30, of which 21 were waited for; matrix products, arithmetic and copies ran while one was open for 10% of the time, Pallas kernels for 0%

commit v1 on v0

v1 whole, which is shorter than its diff:
```python
import functools

import jax
import jax.numpy as jnp
from jax import lax
from jax.experimental import pallas as pl
from jax.experimental.pallas import tpu as pltpu
from jax.sharding import PartitionSpec as P

BLK = 64
LAYERS = 2
EPS = 1e-06
NEG = -1e30
BF = jnp.bfloat16
F32 = jnp.float32
MESH = pl.DeviceIdType.MESH


def nn(a, b):
    return lax.dot_general(a, b, (((1,), (0,)), ((), ())), preferred_element_type=F32)


def nt(a, b):
    return lax.dot_general(a, b, (((1,), (1,)), ((), ())), preferred_element_type=F32)


def tn(a, b):
    return lax.dot_general(a, b, (((0,), (0,)), ((), ())), preferred_element_type=F32)


def normalise(z):
    mu = jnp.mean(z, axis=-1, keepdims=True)
    c = z - mu
    rs = lax.rsqrt(jnp.mean(c * c, axis=-1, keepdims=True) + EPS)
    return c * rs, rs


def norm_back(dn, n, rs):
    return (dn - jnp.mean(dn, axis=-1, keepdims=True) - n * jnp.mean(dn * n, axis=-1, keepdims=True)) * rs


def low_lanes(shape):
    return lax.broadcasted_iota(jnp.int32, shape, len(shape) - 1) % 128 < 64


def body(
    direct, nz, rw,
    wl, sm, xin, cot, segk, segqm,
    act, dxo, gout, gsm,
    W, SG, SV, XA, KV, QP, OO, LSE, H1, DG, G, N1, N2, RS1, RS2, XR, DZ, EB,
    PB, rsib, ry, DXP, xsib, xy, xz, ACC, MX, LS, DKV, DU, DQ, DO, DEL, XRV, ZRV, SL, St1, St2, Sz, Sx,
    wg_s, wg_r, ax_s, ax_r, a4_s, a4_r, r4_s, r4_r, r16_s, r16_r, g_s, g_r, s_s, s_r,
):
    d, z, t = lax.axis_index("dp"), lax.axis_index("seq"), lax.axis_index("tensor")
    c = t % 2
    y = t // 2
    sib, yp = 2 * y + (1 - c), 2 * (1 - y) + c
    DM = XA.shape[2]
    TL = xin.shape[0]
    QT = TL // 4
    HALF = TL // 2
    dsib, dyp = (d, z, sib), (d, z, yp)
    zk = [lax.rem(z + k, nz) for k in range(nz)]
    zm = [lax.rem(z - k + nz, nz) for k in range(nz)]
    pending = []

    bar = pltpu.get_barrier_semaphore()
    peers = [dsib, dyp] + [(d, zk[k], t) for k in range(1, nz)]
    if direct:
        dx_dev = (1 - d, z, t)
        peers.append(dx_dev)
    for p in peers:
        pl.semaphore_signal(bar, inc=1, device_id=p, device_id_type=MESH)
    pl.semaphore_wait(bar, len(peers))

    def send(src, dst, ss, rs, dev):
        cp = pltpu.make_async_remote_copy(src_ref=src, dst_ref=dst, send_sem=ss, recv_sem=rs, device_id=dev, device_id_type=MESH)
        cp.start()
        return cp

    def rows(start, n):
        return pl.ds(pl.multiple_of(start, n if n % 16 == 0 else 16), n)

    own = rows(t * QT, QT)

    wz = {}
    wx = {}
    if direct:
        slot = d * nz + z

        def w_z(p):
            if p == 6:
                SG[slot] = sm[...]
                src = sm
                dst = SG.at[slot]
            else:
                W[p, rows(slot * rw, rw), :] = wl[p]
                src = wl.at[p]
                dst = W.at[p, rows(slot * rw, rw), :]
            wz[p] = [send(src, dst, wg_s.at[p, k], wg_r.at[p, k], (d, zk[k], t)) for k in range(1, nz)]

        def w_x(p):
            for cp in wz[p]:
                cp.wait_recv()
            if p == 6:
                ref = SG.at[pl.ds(d * nz, nz)]
            else:
                ref = W.at[p, rows(d * (nz * rw), nz * rw), :]
            wx[p] = send(ref, ref, wg_s.at[p, 0], wg_r.at[p, 0], dx_dev)

        def w_fin(p):
            wx[p].wait_recv()

        def w_sent(p):
            for cp in wz[p]:
                cp.wait_send()
            wx[p].wait_send()
    else:

        def w_z(p):
            if p == 6:
                SV[...] = sm[...]
            else:
                W[p] = wl[p]

        def w_x(p):
            pass

        w_fin = w_sent = w_x

    def ag4(i, ref):
        own_rows = ref.at[own, :]
        cps = [
            send(own_rows, own_rows, a4_s.at[i, 0], a4_r.at[i, 0], dsib),
            send(own_rows, own_rows, a4_s.at[i, 1], a4_r.at[i, 1], dyp),
        ]

        def fin():
            cps[1].wait_recv()
            r = ref.at[rows(yp * QT, QT), :]
            cps.append(send(r, r, a4_s.at[i, 2], a4_r.at[i, 2], dsib))
            cps[0].wait_recv()
            cps[2].wait_recv()

        def sent():
            for cp in cps:
                cp.wait_send()

        return fin, sent

    def rs4(i, part, filler=None):
        r0 = [(1 - y) * HALF, y * HALF]
        cps = []
        for k in range(2):
            PB[rows(r0[k], HALF), :] = part(rows(r0[k], HALF)).astype(BF)
            cps.append(send(PB.at[rows(r0[k] + (1 - c) * QT, QT), :], rsib.at[k], r4_s.at[i, k], r4_r.at[i, k], dsib))
            if k == 0:
                cps[0].wait_recv()
                mine = rows(r0[0] + c * QT, QT)
                PB[mine, :] = (PB[mine, :].astype(F32) + rsib[0].astype(F32)).astype(BF)
                ycp = send(PB.at[mine, :], ry, r4_s.at[i, 2], r4_r.at[i, 2], dyp)
        if filler is not None:
            filler()
        cps[1].wait_recv()
        ycp.wait_recv()
        total = PB[own, :].astype(F32) + rsib[1].astype(F32) + ry[...].astype(F32)
        cps[0].wait_send()
        cps[1].wait_send()
        ycp.wait_send()
        return total

    def xgather(l):
        st = {}

        def src_rows(j, q):
            return XA.at[l, rows(zm[j] * TL + q * QT, QT), :]

        def start():
            r = src_rows(0, t)
            if l > 0:
                st["c", 0] = send(r, r, ax_s.at[l, nz], ax_r.at[l, nz], dsib)
                st["y", 0] = send(r, r, ax_s.at[l, 2 * nz], ax_r.at[l, 2 * nz], dyp)
            for k in range(1, nz):
                st["z", k] = send(r, r, ax_s.at[l, k], ax_r.at[l, k], (d, zk[k], t))

        def mid(j):
            st["z", j].wait_recv()
            r = src_rows(j, t)
            st["y", j] = send(r, r, ax_s.at[l, 2 * nz + j], ax_r.at[l, 2 * nz + j], dyp)
            st["c", j] = send(r, r, ax_s.at[l, nz + j], ax_r.at[l, nz + j], dsib)

        def fwd(j):
            st["y", j].wait_recv()
            r = src_rows(j, yp)
            st["c2", j] = send(r, r, ax_s.at[l, 3 * nz + j], ax_r.at[l, 3 * nz + j], dsib)

        def fin(j):
            st["c", j].wait_recv()
            st["c2", j].wait_recv()

        def sent():
            for cp in st.values():
                cp.wait_send()

        return start, mid, fwd, fin, sent

    def small(l, r):
        return SV[l, r : r + 1, :]

    def kv_proj(l, j):
        r = rows(zm[j] * TL, TL)
        bias = SV[l, 8:9, 0:384]
        KV[l, r, :] = (nn(XA[l, r, :], W[3 * l, :, 0:384]) + bias).astype(BF)

    def q_proj(l):
        bias = SV[l, 7:8, 0:256]
        q = (nn(XA[l, rows(z * TL, TL), :], W[3 * l, :, 384:640]) + bias).astype(BF).astype(F32) * 0.125
        a, b = q[:, 0:128], q[:, 128:256]
        lo = low_lanes(a.shape)
        QP[l, :, 0:128] = jnp.where(lo, a, 0.0).astype(BF)
        QP[l, :, 128:256] = jnp.where(lo, 0.0, a).astype(BF)
        QP[l, :, 256:384] = jnp.where(lo, b, 0.0).astype(BF)

    nb = TL // BLK

    def masked_scores(l, h, hl, r, j):
        kv = KV[l, r, pl.ds(hl, 128)]
        s = nt(kv, QP[l, :, pl.ds(hl, 128)])
        sq = segqm[h, pl.ds(pl.multiple_of(zm[j] * nb, nb), nb), :]
        sk = segk[r, :]
        parts = []
        for b in range(nb):
            skb = jnp.concatenate([sk[b * BLK : (b + 1) * BLK]] * (TL // 128), axis=1)
            parts.append(jnp.where(skb == sq[b : b + 1], s[b * BLK : (b + 1) * BLK], NEG))
        return kv, jnp.concatenate(parts, axis=0)

    def attend(l, j):
        r = rows(zm[j] * TL, TL)

        def head(h, carry):
            hl = pl.multiple_of(h * 128, 128)
            kv, s = masked_scores(l, h, hl, r, j)
            top = jnp.max(s, axis=0, keepdims=True)
            if j > 0:
                before = MX[h]
                top = jnp.maximum(before, top)
            e = jnp.exp(s - top)
            total = jnp.sum(e, axis=0, keepdims=True)
            o = tn(kv, e.astype(BF))
            if j > 0:
                a = jnp.exp(before - top)
                total = total + LS[h] * a
                o = o + ACC[h] * a
            MX[h] = top
            LS[h] = total
            ACC[h] = o
            return carry

        lax.fori_loop(0, 3, head, 0)

    def attend_end(l):
        o = []
        for h in range(3):
            LSE[3 * l + h] = MX[h] + jnp.log(LS[h])
            o.append((ACC[h] / LS[h]).T)
        lo = low_lanes(o[0].shape)
        OO[l, :, 0:128] = jnp.where(lo, 0.0, o[2]).astype(BF)
        OO[l, :, 128:256] = jnp.where(lo, o[1], o[0]).astype(BF)

    def gelu_parts(u):
        k = 0.7978845608028654
        th = jnp.tanh(k * (u + 0.044715 * u * u * u))
        g = 0.5 * u * (1.0 + th)
        dg = 0.5 * (1.0 + th) + 0.5 * u * (1.0 - th * th) * (k * (1.0 + 3 * 0.044715 * u * u))
        return g, dg

    def forward(l, bg):
        start, mid, fwd, fin, sent = xg[l]
        if l > 0:
            start()
            mid(1)
            fwd(0)
            fin(0)
        q_proj(l)
        kv_proj(l, 0)
        if l > 0:
            mid(2)
        attend(l, 0)
        bg[0]()
        if l > 0:
            mid(3)
            fwd(1)
        for j in range(1, nz):
            fin(j)
            kv_proj(l, j)
            if j + 1 < nz:
                if l > 0:
                    fwd(j + 1)
            attend(l, j)
            if j == nz - 2:
                bg[1]()
        attend_end(l)
        sent()
        wo = W[3 * l, :, 512:768]
        r = rs4(3 * l, lambda rr: nt(OO[l, rr, :], wo))
        z1 = XR[...] + r + small(l, 0)
        n1, rs1 = normalise(z1)
        N1[l] = n1
        RS1[l] = rs1
        h1 = n1 * small(l, 4) + small(l, 1)
        H1[l, own, :] = h1.astype(BF)
        XR[...] = h1
        done, gone = ag4(4 * l, H1.at[l])
        bg[2]()
        done()
        w_fin(3 * l + 1)
        w_fin(3 * l + 2)

        def ffn(rr):
            u = nn(H1[l, rr, :], W[3 * l + 1]) + small(l, 6)
            g, dg = gelu_parts(u)
            DG[l, rr, :] = dg.astype(BF)
            gb = g.astype(BF)
            G[l, rr, :] = gb
            return nt(gb, W[3 * l + 2])

        r = rs4(3 * l + 1, ffn, gone)
        bg[3]()
        z2 = XR[...] + r + small(l, 2)
        n2, rs2 = normalise(z2)
        N2[l] = n2
        RS2[l] = rs2
        out = n2 * small(l, 5) + small(l, 3)
        XR[...] = out
        return out.astype(BF)

    gx = {}
    gz = {}

    if direct:

        def g_start(p):
            ref = W.at[p, rows((1 - d) * (nz * rw), nz * rw), :]
            gx[p] = send(ref, XRV.at[p], g_s.at[p, 0], g_r.at[p, 0], dx_dev)

        def g_mid(p):
            gx[p].wait_recv()
            r = rows(d * (nz * rw), nz * rw)
            W[p, r, :] = (W[p, r, :].astype(F32) + XRV[p].astype(F32)).astype(BF)
            gz[p] = [
                send(W.at[p, rows((d * nz + zk[k]) * rw, rw), :], ZRV.at[p, k - 1], g_s.at[p, k], g_r.at[p, k], (d, zk[k], t))
                for k in range(1, nz)
            ]

        def g_fin(p):
            for cp in gz[p]:
                cp.wait_recv()
            tot = W[p, rows((d * nz + z) * rw, rw), :].astype(F32)
            for k in range(nz - 1):
                tot = tot + ZRV[p, k].astype(F32)
            gout[p] = tot
            pending.append(gx[p])
            pending.extend(gz[p])
    else:

        def g_start(p):
            gout[p] = W[p]

        def g_mid(p):
            pass

        g_fin = g_mid

    def backward(l, bg):
        dy = DZ[...]
        n2 = N2[l]
        SL[l, 3:4, :] = jnp.sum(dy, axis=0, keepdims=True)
        SL[l, 5:6, :] = jnp.sum(dy * n2, axis=0, keepdims=True)
        dz2 = norm_back(dy * small(l, 5), n2, RS2[l])
        SL[l, 2:3, :] = jnp.sum(dz2, axis=0, keepdims=True)
        DZ[...] = dz2
        EB[2 * l + 1, own, :] = dz2.astype(BF)
        done, gone = ag4(4 * l + 2, EB.at[2 * l + 1])
        bg[0]()
        done()

        def ffn_back(rr):
            dgm = nn(EB[2 * l + 1, rr, :], W[3 * l + 2])
            du = (dgm * DG[l, rr, :].astype(F32)).astype(BF)
            DU[rr, :] = du
            return nt(du, W[3 * l + 1])

        def fill():
            gone()
            w_sent(3 * l + 2)
            w_sent(3 * l + 1)
            W[3 * l + 2] = tn(EB[2 * l + 1], G[l]).astype(BF)
            g_start(3 * l + 2)
            W[3 * l + 1] = tn(H1[l], DU[...]).astype(BF)
            g_start(3 * l + 1)
            SL[l, 6:7, :] = jnp.sum(DU[...].astype(F32), axis=0, keepdims=True)

        r = rs4(3 * l + 2, ffn_back, fill)
        dh1 = DZ[...] + r
        n1 = N1[l]
        SL[l, 1:2, :] = jnp.sum(dh1, axis=0, keepdims=True)
        SL[l, 4:5, :] = jnp.sum(dh1 * n1, axis=0, keepdims=True)
        dz1 = norm_back(dh1 * small(l, 4), n1, RS1[l])
        SL[l, 0:1, :] = jnp.sum(dz1, axis=0, keepdims=True)
        DZ[...] = dz1
        EB[2 * l, own, :] = dz1.astype(BF)
        done, gone1 = ag4(4 * l + 3, EB.at[2 * l])
        bg[1]()
        done()
        doo = nn(EB[2 * l], W[3 * l, :, 512:768]).astype(BF).astype(F32)
        lo = low_lanes((TL, 128))
        da, db = doo[:, 0:128], doo[:, 128:256]
        DO[:, 0:128] = jnp.where(lo, 0.0, db).astype(BF)
        DO[:, 128:256] = jnp.where(lo, db, 0.0).astype(BF)
        DO[:, 256:384] = jnp.where(lo, 0.0, da).astype(BF)
        prod = (doo * OO[l].astype(F32)).T
        DEL[0] = jnp.sum(prod[192:256], axis=0, keepdims=True)
        DEL[1] = jnp.sum(prod[128:192], axis=0, keepdims=True)
        DEL[2] = jnp.sum(prod[64:128], axis=0, keepdims=True)

        xs = {}
        order = list(range(1, nz)) + [0]

        def attend_back(j, first):
            r = rows(zm[j] * TL, TL)

            def head(h, carry):
                hl = pl.multiple_of(h * 128, 128)
                kv, s = masked_scores(l, h, hl, r, j)
                q = QP[l, :, pl.ds(hl, 128)]
                do = DO[:, pl.ds(hl, 128)]
                p = jnp.exp(s - LSE[3 * l + h])
                dp = nt(kv, do)
                ds = (p * (dp - DEL[h])).astype(BF)
                DKV[r, pl.ds(hl, 128)] = (nn(ds, q) + nn(p.astype(BF), do)).astype(BF)
                dq = tn(kv, ds)
                if first:
                    ACC[h] = dq
                else:
                    ACC[h] = ACC[h] + dq
                return carry

            lax.fori_loop(0, 3, head, 0)

        def dx_parts(j):
            for k in range(2):
                r0 = [(1 - y) * HALF, y * HALF][k]
                v = nt(DKV[rows(zm[j] * TL + r0, HALF), :], W[3 * l, :, 0:384])
                if j == 0:
                    v = v + nt(DQ[rows(r0, HALF), :], W[3 * l, :, 384:640])
                DXP[j, rows(r0, HALF), :] = v.astype(BF)
                xs["c", j, k] = send(DXP.at[j, rows(r0 + (1 - c) * QT, QT), :], xsib.at[j, k], r16_s.at[l, 3 * j + k], r16_r.at[l, 3 * j + k], dsib)

        def dx_y(j):
            xs["c", j, 0].wait_recv()
            mine = rows(yp * QT, QT)
            DXP[j, mine, :] = (DXP[j, mine, :].astype(F32) + xsib[j, 0].astype(F32)).astype(BF)
            xs["y", j] = send(DXP.at[j, mine, :], xy.at[j], r16_s.at[l, 3 * j + 2], r16_r.at[l, 3 * j + 2], dyp)

        def dx_z(j):
            xs["c", j, 1].wait_recv()
            xs["y", j].wait_recv()
            tot = DXP[j, own, :].astype(F32) + xsib[j, 1].astype(F32) + xy[j].astype(F32)
            if j == 0:
                return tot
            DXP[j, own, :] = tot.astype(BF)
            xs["z", j] = send(DXP.at[j, own, :], xz.at[l, j - 1], r16_s.at[l, 3 * nz + j - 1], r16_r.at[l, 3 * nz + j - 1], (d, zm[j], t))

        for i, j in enumerate(order):
            attend_back(j, i == 0)
            if i >= 2:
                dx_z(order[i - 2])
            if i == 1:
                bg[2]()
            if j == 0:
                a01 = ACC[0]
                hi = lax.broadcasted_iota(jnp.int32, a01.shape, 0) < 64
                DQ[:, 0:128] = (jnp.where(hi, a01, ACC[1]).T * 0.125).astype(BF)
                DQ[:, 128:256] = (jnp.where(hi, ACC[2], 0.0).T * 0.125).astype(BF)
            dx_parts(j)
            dx_y(j)
        dx_z(order[nz - 2])
        gone1()
        w_sent(3 * l)
        xown = XA[l, rows(z * TL, TL), :]
        gq = tn(xown, DQ[...])
        go = tn(EB[2 * l], OO[l])
        gkv = tn(XA[l], DKV[...])
        mine_total = dx_z(0)
        W[3 * l, :, 0:384] = gkv.astype(BF)
        W[3 * l, :, 384:512] = gq[:, 0:128].astype(BF)
        W[3 * l, :, 512:640] = (gq[:, 128:256] + go[:, 0:128]).astype(BF)
        W[3 * l, :, 640:768] = go[:, 128:256].astype(BF)
        g_start(3 * l)
        SL[l, 7:8, 0:384] = jnp.sum(DKV[...].astype(F32), axis=0, keepdims=True)
        SL[l, 7:8, 384:640] = jnp.sum(DQ[...].astype(F32), axis=0, keepdims=True)
        SL[l, 7:8, 640:768] = jnp.zeros((1, 128), F32)
        tot = DZ[...] + mine_total
        for j in range(1, nz):
            xs["z", j].wait_recv()
            tot = tot + xz[l, j - 1].astype(F32)
        DZ[...] = tot
        for cp in xs.values():
            cp.wait_send()
        return tot

    xg = [xgather(0), xgather(1)]
    XA[0, rows(z * TL, TL), :] = xin[...]
    XR[...] = xin[own, :].astype(F32)
    w_z(6)
    xg[0][0]()
    w_z(0)
    for j in range(1, nz):
        xg[0][1](j)
    w_x(6)
    w_x(0)
    w_z(1)
    for j in range(1, nz):
        xg[0][2](j)
    w_fin(6)
    if direct:
        wide = DM - 128
        nslot = SG.shape[0]
        for l in range(LAYERS):
            acc = jnp.zeros((16, DM), F32)
            cmp_ = jnp.zeros((8, DM), F32)
            for s_ in range(nslot):
                piece = jnp.concatenate([SG[s_, l], jnp.zeros((16, wide), F32)], axis=1)
                acc = acc + (pltpu.roll(piece, s_ * rw, 1) if s_ else piece)
                cmp_ = cmp_ + (pltpu.roll(piece[8:16], s_ * (rw // 4), 1) if s_ else piece[8:16])
            bq, bv = cmp_[0:1], cmp_[1:2]
            lane = lax.broadcasted_iota(jnp.int32, (1, DM), 1)
            kvb = jnp.where((lane >= 64) & (lane < 192), pltpu.roll(bv, 64, 1), 0.0) + jnp.where(
                (lane >= 320) & (lane < 384), pltpu.roll(bv, 192, 1), 0.0
            )
            SV[l, 0:8, :] = acc[0:8]
            SV[l, 7:8, :] = bq
            SV[l, 8:9, :] = kvb
    w_fin(0)

    def after_first():
        w_x(1)
        w_z(2)

    def b2():
        w_x(2)
        w_z(3)

    def b3():
        pass

    def b4():
        w_x(3)
        w_z(4)

    x1 = forward(0, [after_first, b2, b3, b4])
    XA[1, rows(z * TL + t * QT, QT), :] = x1
    w_fin(3)

    def c1():
        w_x(4)
        w_z(5)

    def c2():
        w_x(5)

    nop = lambda: None
    x2 = forward(1, [c1, c2, nop, nop])
    EB[0, own, :] = x2
    act_done, act_sent = ag4(1, EB.at[0])
    DZ[...] = cot[own, :].astype(F32)

    def act_end():
        act_done()
        act[...] = EB[0]
        act_sent()

    def m5():
        g_mid(5)

    def m4():
        g_mid(4)

    backward(1, [act_end, m5, m4])

    def m3():
        g_mid(3)
        g_fin(5)

    def m2():
        g_mid(2)
        g_fin(4)

    def m1():
        g_mid(1)
        g_fin(3)

    dx = backward(0, [m3, m2, m1])
    EB[3, own, :] = dx.astype(BF)
    dx_done, dx_sent = ag4(5, EB.at[3])

    cps = [send(SL, St1, s_s.at[0], s_r.at[0], dsib)]
    cps[0].wait_recv()
    cps[0].wait_send()
    keep = lax.broadcasted_iota(jnp.int32, SL.shape, 1) < 6
    SL[...] = SL[...] + jnp.where(keep, St1[...], 0.0)
    cps.append(send(SL, St2, s_s.at[1], s_r.at[1], dyp))
    cps[1].wait_recv()
    cps[1].wait_send()
    SL[...] = SL[...] + jnp.where(keep, St2[...], 0.0)
    zc = [send(SL, Sz.at[k - 1], s_s.at[1 + k], s_r.at[1 + k], (d, zk[k], t)) for k in range(1, nz)]
    for cp in zc:
        cp.wait_recv()
    for cp in zc:
        cp.wait_send()
    tot = SL[...]
    for k in range(nz - 1):
        tot = tot + Sz[k]
    g_mid(0)
    if direct:
        SL[...] = tot
        xc = send(SL, Sx, s_s.at[1 + nz], s_r.at[1 + nz], dx_dev)
        xc.wait_recv()
        xc.wait_send()
        tot = tot + Sx[...]
    gsm[...] = tot
    g_fin(2)
    g_fin(1)
    dx_done()
    dxo[...] = EB[3]
    dx_sent()
    g_fin(0)
    w_sent(6)
    for cp in pending:
        cp.wait_send()


def shards(dp, nz, nt_, x_in, cotangent, segment_ids, random_blocks, wqkv, wo, w1, w2, qv_bias, mid_bias, shifts, gains):
    rw = wqkv.shape[1]
    direct = dp == 2 and rw % 16 == 0
    TL, DM = x_in.shape[1], x_in.shape[2]
    length = segment_ids.shape[1]
    z = lax.axis_index("seq")
    slot = lax.axis_index("dp") * nz + z
    axes = ("dp", "seq")

    qw, kw, vw = [wqkv[:, :, i, :].reshape(LAYERS, rw, 3, 64) for i in range(3)]
    ot = wo.transpose(0, 2, 1).reshape(LAYERS, rw, 3, 64)
    attn = jnp.concatenate(
        [kw[:, :, 0], vw[:, :, 0], vw[:, :, 1], kw[:, :, 1], kw[:, :, 2], vw[:, :, 2],
         qw[:, :, 0], qw[:, :, 1], qw[:, :, 2], ot[:, :, 2], ot[:, :, 1], ot[:, :, 0]], axis=2)
    wl = jnp.stack([attn, w1, w2.transpose(0, 2, 1)], axis=1).astype(BF).reshape(3 * LAYERS, rw, DM)

    def low(v):
        return v.astype(BF).astype(F32)

    if direct:
        def lanes(v):
            return jnp.pad(low(v), ((0, 0), (0, 0), (0, 128 - v.shape[2])))
        sm = jnp.concatenate(
            [lanes(shifts), lanes(gains), lanes(mid_bias), jnp.zeros((LAYERS, 1, 128), F32), lanes(qv_bias[:, :, 0]),
             jnp.zeros((LAYERS, 6, 128), F32)], axis=1)
    else:
        wl = lax.all_gather(wl, axes, axis=1, tiled=True)
        sh = lax.all_gather(shifts.astype(BF), axes, axis=2, tiled=True).astype(F32)
        ga = lax.all_gather(gains.astype(BF), axes, axis=2, tiled=True).astype(F32)
        mb = lax.all_gather(mid_bias.astype(BF), axes, axis=2, tiled=True).astype(F32)
        qv = lax.all_gather(qv_bias[:, :, 0].astype(BF), axes, axis=2, tiled=True).astype(F32)
        bq, bv = qv[:, 0:1], qv[:, 1:2]
        gap = jnp.zeros((LAYERS, 1, 64), F32)
        kvb = jnp.concatenate([gap, bv[..., 0:128], gap, gap, bv[..., 128:192]], axis=2)
        fit = lambda v: jnp.pad(v, ((0, 0), (0, 0), (0, DM - v.shape[2])))
        sm = jnp.concatenate([sh, ga, mb, fit(bq), fit(kvb), jnp.zeros((LAYERS, 7, DM), F32)], axis=1)

    nblk = length // BLK
    nb = TL // BLK
    seg = segment_ids[0]
    segk = jnp.broadcast_to(seg[:, None], (length, 128))
    rnd = lax.dynamic_slice_in_dim(random_blocks[0], z * nb, nb, axis=1)
    qi = (z * nb + jnp.arange(nb, dtype=jnp.int32))[None, :, None]
    kj = jnp.arange(nblk, dtype=jnp.int32)[None, None, :]
    ok = (jnp.abs(qi - kj) <= 1) | (kj == 0) | (kj == nblk - 1)
    ok = ok | jnp.any(rnd[:, :, :, None] == kj[:, :, None, :], axis=2)
    segq = lax.dynamic_slice_in_dim(seg, z * TL, TL)
    heads = rnd.shape[0]
    segqm = jnp.where(ok.transpose(0, 2, 1)[:, :, :, None], segq.reshape(1, 1, nb, BLK), -1).reshape(heads, nblk, TL)

    QT = TL // 4
    L = LAYERS
    nslot = dp * nz if direct else 1
    grw = rw if direct else DM
    vm = pl.BlockSpec(memory_space=pltpu.VMEM)
    dma = pltpu.SemaphoreType.DMA
    xr = nz * rw if direct else 16
    scratch = [
        pltpu.VMEM((3 * L, DM, DM), BF),
        pltpu.VMEM((nslot, L, 16, 128), F32),
        pltpu.VMEM((L, 16, DM), F32),
        pltpu.VMEM((L, length, DM), BF),
        pltpu.VMEM((L, length, 384), BF),
        pltpu.VMEM((L, TL, 384), BF),
        pltpu.VMEM((L, TL, 256), BF),
        pltpu.VMEM((3 * L, 1, TL), F32),
        pltpu.VMEM((L, TL, DM), BF),
        pltpu.VMEM((L, TL, DM), BF),
        pltpu.VMEM((L, TL, DM), BF),
        pltpu.VMEM((L, QT, DM), F32),
        pltpu.VMEM((L, QT, DM), F32),
        pltpu.VMEM((L, QT, 1), F32),
        pltpu.VMEM((L, QT, 1), F32),
        pltpu.VMEM((QT, DM), F32),
        pltpu.VMEM((QT, DM), F32),
        pltpu.VMEM((2 * L, TL, DM), BF),
        pltpu.VMEM((TL, DM), BF),
        pltpu.VMEM((2, QT, DM), BF),
        pltpu.VMEM((QT, DM), BF),
        pltpu.VMEM((nz, TL, DM), BF),
        pltpu.VMEM((nz, 2, QT, DM), BF),
        pltpu.VMEM((nz, QT, DM), BF),
        pltpu.VMEM((L, nz - 1, QT, DM), BF),
        pltpu.VMEM((3, 128, TL), F32),
        pltpu.VMEM((3, 1, TL), F32),
        pltpu.VMEM((3, 1, TL), F32),
        pltpu.VMEM((length, 384), BF),
        pltpu.VMEM((TL, DM), BF),
        pltpu.VMEM((TL, 256), BF),
        pltpu.VMEM((TL, 384), BF),
        pltpu.VMEM((3, 1, TL), F32),
        pltpu.VMEM((3 * L, xr, DM) if direct else (1, 16, 128), BF),
        pltpu.VMEM((3 * L, nz - 1, rw, DM) if direct else (1, 1, 16, 128), BF),
        pltpu.VMEM((L, 8, DM), F32),
        pltpu.VMEM((L, 8, DM), F32),
        pltpu.VMEM((L, 8, DM), F32),
        pltpu.VMEM((nz - 1, L, 8, DM), F32),
        pltpu.VMEM((L, 8, DM), F32),
        dma((7, nz)), dma((7, nz)),
        dma((L, 4 * nz)), dma((L, 4 * nz)),
        dma((8, 3)), dma((8, 3)),
        dma((6, 3)), dma((6, 3)),
        dma((L, 4 * nz)), dma((L, 4 * nz)),
        dma((6, nz)), dma((6, nz)),
        dma((2 + nz,)), dma((2 + nz,)),
    ]
    act, dx, gout, gsm = pl.pallas_call(
        functools.partial(body, direct, nz, rw),
        out_shape=(
            jax.ShapeDtypeStruct((TL, DM), BF),
            jax.ShapeDtypeStruct((TL, DM), BF),
            jax.ShapeDtypeStruct((3 * L, grw, DM), F32 if direct else BF),
            jax.ShapeDtypeStruct((L, 8, DM), F32),
        ),
        in_specs=[vm] * 6,
        out_specs=(vm,) * 4,
        scratch_shapes=scratch,
        compiler_params=pltpu.CompilerParams(collective_id=0, has_side_effects=True, vmem_limit_bytes=60 * 2**20),
        name="encoder",
    )(wl, sm, x_in[0], cotangent[0], segk, segqm)

    if not direct:
        gout = lax.psum_scatter(gout.astype(F32), axes, scatter_dimension=1, tiled=True)
        gsm = lax.psum(gsm, "dp")
    gout = gout.reshape(L, 3, rw, DM)
    ga, g1, g2 = gout[:, 0], gout[:, 1], gout[:, 2]
    pc = [ga[:, :, i * 64 : (i + 1) * 64] for i in range(12)]
    gq = jnp.concatenate([pc[6], pc[7], pc[8]], axis=2)
    gk = jnp.concatenate([pc[0], pc[3], pc[4]], axis=2)
    gv = jnp.concatenate([pc[1], pc[2], pc[5]], axis=2)
    go = jnp.concatenate([pc[11], pc[10], pc[9]], axis=2).transpose(0, 2, 1)
    sl = lax.dynamic_slice_in_dim(gsm[:, 0:7], slot * rw, rw, axis=2)
    dbq = gsm[:, 7, 384:576]
    dbv = jnp.concatenate([gsm[:, 7, 64:192], gsm[:, 7, 320:384]], axis=1)
    qv = lax.dynamic_slice_in_dim(jnp.stack([dbq, dbv], axis=1), slot * (rw // 4), rw // 4, axis=2)
    return (
        act[None],
        dx[None].astype(F32),
        jnp.stack([gq, gk, gv], axis=2),
        go,
        g1,
        g2.transpose(0, 2, 1),
        qv[:, :, None, :],
        sl[:, 6:7],
        sl[:, 0:4],
        sl[:, 4:6],
    )


def solution(mesh):
    both = ("dp", "seq")
    weights = (
        P(None, both, None, "tensor"),
        P(None, "tensor", both),
        P(None, both, "tensor"),
        P(None, "tensor", both),
        P(None, None, "tensor", both),
        P(None, "tensor", both),
        P(None, None, both),
        P(None, None, both),
    )
    tokens = P("dp", "seq", None)
    in_specs = (tokens, tokens, P("dp", None), P("dp", "tensor", None, None)) + weights
    out_specs = (tokens, tokens) + weights
    fn = functools.partial(shards, mesh.shape["dp"], mesh.shape["seq"], mesh.shape["tensor"])
    return jax.shard_map(fn, mesh=mesh, in_specs=in_specs, out_specs=out_specs, check_vma=False)
```

time: 1940 us -> 359 us (0.19)
  waiting for transfers between devices: 1040 us -> 0 us
  blocking collectives: 449 us -> 0 us
  Pallas kernels: 0 us -> 332 us
  local copies, waits for them, and re-layouts: 246 us -> 19.2 us
  matrix products: 110 us -> 0 us
  other arithmetic: 58.4 us -> 3.21 us
    unnamed x40 -> x0, waiting for transfers between devices: 561 us -> none
    all_gather x14 -> x0, blocking collectives: 409 us -> none  [the longest x2 80.6 us: fetch_layer(): lax.all_gather(query_key_value_weight, ('dp', 'seq'), axis=0, tiled=True)]
    pallas_call x0 -> x1, Pallas kernels: none -> 332 us  [shards(): pl.pallas_call(functools.partial(body, direct, nz, rw), out_shape=(jax.Sh...]
    reduce_scatter x8 -> x0, waiting for transfers between devices: 320 us -> none  [the longest x2 143 us: reduce_layer(): lax.psum_scatter(g_back, ('dp', 'seq'), scatter_dimension=1, tiled=True)]
    psum x8 -> x0, waiting for transfers between devices: 163 us -> none  [the longest x4 128 us: input_grad_sum(): return lax.psum(terms.astype(jnp.bfloat16), 'tensor').astype(jnp.float32)]
    dot_general x36 -> x0, matrix products: 105 us -> none  [the longest x4 24.6 us: spread_back(): jnp.einsum('shjb,shjkd->shbkd', chooser, per_slot, precision=lax.Precisio...]
    another operation x33 -> x2, local copies, waits for them, and re-layouts: 56.6 us -> 1 us  [the longest x1 0.99 us: shards(): jnp.stack([attn, w1, w2.transpose(0, 2, 1)], axis=1).astype(BF)]
    unnamed x2 -> x0, blocking collectives: 40.1 us -> none
  transfers between devices with their start and end apart: 30 -> 0, of which waited for: 21 -> 0; matrix products, arithmetic and copies ran while one was open for 10% -> 0% of each run, Pallas kernels for 0% -> 0%
where the time goes in v1:
time: 359 us; the launch traced here: 356 us
  Pallas kernels  332 us (92%)
  local copies, waits for them, and re-layouts  19.2 us (5%)
    pallas_call x1, Pallas kernels, shards(): pl.pallas_call(functools.partial(body, direct, nz, rw), out_shape=(jax.Sh...  332 us

profile of v1, /device:TPU:0, one launch (start us, length us, event | category | flops | bytes accessed | tf_op | source)
XLA Modules:
  0.0 355.9 jit_solution(10406901491117934736)
XLA Ops:
  0.6 0.0 copy-start
  0.7 0.0 copy-start.5
  0.7 1.2 fusion.7
  1.9 0.0 copy-start.3
  1.9 0.1 copy.109
  2.0 0.1 copy.110
  2.1 0.1 copy.117
  2.3 0.1 copy.119
  2.4 0.0 copy-start.4
  2.4 0.1 copy.120
  2.5 0.1 copy.111
  2.6 0.1 copy.112
  2.8 0.1 copy.113
  2.9 0.1 copy.114
  3.0 0.1 copy.115
  3.1 0.1 copy.116
  3.2 0.1 copy.118
  3.3 0.0 copy-done.5
  3.4 0.1 copy.121
  3.5 0.1 copy.122
  3.6 0.1 copy.123
  3.7 0.2 concatenate.23
  4.0 0.0 copy-done.3
  4.0 0.0 copy-done.4
  4.1 0.0 copy-start.6
  4.1 0.0 copy-start.9
  4.1 0.0 copy-start.8
  4.1 0.0 copy-start.7
  4.1 0.0 copy-start.10
  4.1 0.1 pad_maximum_fusion
  4.2 1.0 copy.96
  5.2 0.0 copy-done
  5.2 0.1 constant_dynamic-slice_fusion.4
  5.3 0.1 fusion
  5.4 0.1 fusion.2
  5.5 0.1 copy.97
  5.6 0.2 broadcast_in_dim.52
  5.8 0.2 broadcast_in_dim.53
  6.0 0.0 copy-done.6
  6.0 0.7 broadcast_select_fusion.segqm
  6.7 0.0 copy-done.9
  6.7 0.0 copy-done.8
  6.8 0.0 copy-done.7
  6.8 0.0 copy-done.10
  6.9 1.2 concatenate.24.sm
  8.1 1.3 broadcast_in_dim.51.segk
  9.4 332.1 %encoder.1 = (bf16[512,768]{1,0:T(8,128)(2,1)}, bf16[512,768]{1,0:T(8,128)(2,1)}, f32[6,96,768]{2,1,0:T(8,128)}, f32[2,8,768]{2,1,0:T(8,128)}) custom-call(bf16[6,96,768]{2,1,0:T(8,128)(2,1)} %bitcast.71, f32[2,16,128]{2,1,0:T(8,128)} %concatenate.24.sm, bf16[512,768]{1,0:T(8,128)(2,1)} %bitcast.77, bf16[512,768]{1,0:T(8,128)(2,1)} %bitcast.78, ...), custom_call_target="tpu_custom_call" | custom-call | tf_op jit(solution)/shard_map/encoder/pallas_call | solution.py:749
  341.5 0.8 slice.145
  342.3 0.8 slice.146
  343.1 0.8 copy.101
  343.9 0.1 fusion.4
  344.0 0.6 copy.104
  344.6 2.6 slice_bitcast_fusion
  347.2 0.3 copy.124
  347.5 0.7 maximum_bitcast_fusion.2
  348.2 0.0 copy-start.2
  348.3 0.0 copy-start.1
  348.4 1.1 copy.103
  349.4 1.4 constant_dynamic-slice_fusion
  350.8 1.4 constant_dynamic-slice_fusion.2
  352.2 1.4 constant_dynamic-slice_fusion.1
  353.5 0.0 copy-done.2
  353.5 1.3 bitcast_convert_fusion
  354.8 0.9 copy.132
  (31 shorter events, 0.3 us)
Async XLA Ops:
  0.6 4.6 %copy-start = (s32[1,3,32,3]{2,0,3,1:T(1,128)S(1)}, s32[1,3,32,3]{2,0,3,1:T(1,128)}, u32[]{:S(2)}) copy-start(s32[1,3,32,3]{2,0,3,1:T(1,128)} %param.15) | copy-start | bytes 3460
  0.7 2.7 copy-start.5
  1.9 2.1 copy-start.3
  2.4 1.6 copy-start.4
  4.1 1.9 copy-start.6
  4.1 2.6 copy-start.9
  4.1 2.7 copy-start.8
  4.1 2.7 copy-start.7
  4.1 2.7 copy-start.10
  348.2 5.3 %copy-start.2 = (bf16[512,768]{1,0:T(8,128)(2,1)S(1)}, bf16[512,768]{1,0:T(8,128)(2,1)}, u32[]{:S(2)}) copy-start(bf16[512,768]{1,0:T(8,128)(2,1)} %get-tuple-element.15) | copy-start | bytes 2359300
  348.3 6.5 %copy-start.1 = (bf16[512,768]{1,0:T(8,128)(2,1)S(1)}, bf16[512,768]{1,0:T(8,128)(2,1)}, u32[]{:S(2)}) copy-start(bf16[512,768]{1,0:T(8,128)(2,1)} %get-tuple-element.14) | copy-start | bytes 2359300

commit v2 on v1

--- a/solution.py
+++ b/solution.py
@@ -61,7 +61,10 @@
     HALF = TL // 2
     dsib, dyp = (d, z, sib), (d, z, yp)
     zk = [lax.rem(z + k, nz) for k in range(nz)]
-    zm = [lax.rem(z - k + nz, nz) for k in range(nz)]
+    upper = z // 2
+    edge = (1 - z) * (1 - upper) + (z - 2) * upper
+    inner = 1 - edge
+    ck = [z] + [o + upper * (nz - 1 - 2 * o) for o in (edge, 2, 3)]
     pending = []
 
     bar = pltpu.get_barrier_semaphore()
@@ -83,132 +86,200 @@
 
     own = rows(t * QT, QT)
 
-    wz = {}
-    wx = {}
+    def copy_to(src, dst, ss, rs, dev):
+        return pltpu.make_async_remote_copy(src_ref=src, dst_ref=dst, send_sem=ss, recv_sem=rs, device_id=dev, device_id_type=MESH)
+
     if direct:
         slot = d * nz + z
 
-        def w_z(p):
+        def w_ref(p, k):
+            if p == 6:
+                return SG.at[d * nz + k]
+            return W.at[p, rows((d * nz + k) * rw, rw), :]
+
+        def w_own(p):
+            src = sm if p == 6 else wl.at[p]
+            dst = w_ref(p, z)
+            out = []
+            for i, step in enumerate((1, 2, -1, -2)):
+                ok = z + step < nz if step > 0 else z + step >= 0
+                out.append((ok, copy_to(src, dst, wg_s.at[p, i], wg_r.at[p, z], (d, z + step, t))))
+            return out
+
+        def w_over(p, k):
+            return copy_to(w_ref(p, k), w_ref(p, k), wg_s.at[p, 5 + k], wg_r.at[p, nz + k], dx_dev)
+
+        def w_hop(p):
+            return copy_to(w_ref(p, ck[3]), w_ref(p, ck[3]), wg_s.at[p, 4], wg_r.at[p, ck[3]], (d, nz - 1 - ck[3], t))
+
+        def w_wait(p, k):
+            copy_to(w_ref(p, k), w_ref(p, k), wg_s.at[p, 4], wg_r.at[p, k], dx_dev).wait_recv()
+
+        def w_a(p):
             if p == 6:
                 SG[slot] = sm[...]
-                src = sm
-                dst = SG.at[slot]
             else:
                 W[p, rows(slot * rw, rw), :] = wl[p]
-                src = wl.at[p]
-                dst = W.at[p, rows(slot * rw, rw), :]
-            wz[p] = [send(src, dst, wg_s.at[p, k], wg_r.at[p, k], (d, zk[k], t)) for k in range(1, nz)]
-
-        def w_x(p):
-            for cp in wz[p]:
-                cp.wait_recv()
-            if p == 6:
-                ref = SG.at[pl.ds(d * nz, nz)]
-            else:
-                ref = W.at[p, rows(d * (nz * rw), nz * rw), :]
-            wx[p] = send(ref, ref, wg_s.at[p, 0], wg_r.at[p, 0], dx_dev)
+            for ok, cp in w_own(p):
+                pl.when(ok)(cp.start)
+
+        def w_o(p):
+            src = sm if p == 6 else wl.at[p]
+            copy_to(src, w_ref(p, z), wg_s.at[p, 5 + z], wg_r.at[p, nz + z], dx_dev).start()
+
+        def w_b(p):
+            @pl.when(inner == 1)
+            def _():
+                w_wait(p, ck[3])
+                w_hop(p).start()
+
+        def w_c(p):
+            for k in ck[1:3]:
+                w_wait(p, k)
+                w_over(p, k).start()
+
+        def w_d(p):
+            @pl.when(edge == 1)
+            def _():
+                w_wait(p, ck[3])
+
+            w_over(p, ck[3]).start()
 
         def w_fin(p):
-            wx[p].wait_recv()
+            for k in range(nz):
+                w_over(p, k).wait_recv()
 
         def w_sent(p):
-            for cp in wz[p]:
-                cp.wait_send()
-            wx[p].wait_send()
+            for ok, cp in w_own(p):
+                pl.when(ok)(cp.wait_send)
+
+            @pl.when(inner == 1)
+            def _():
+                w_hop(p).wait_send()
+
+            for k in ck:
+                w_over(p, k).wait_send()
     else:
 
-        def w_z(p):
+        def w_a(p):
             if p == 6:
                 SV[...] = sm[...]
             else:
                 W[p] = wl[p]
 
-        def w_x(p):
+        def w_b(p):
             pass
 
-        w_fin = w_sent = w_x
+        w_o = w_c = w_d = w_fin = w_sent = w_b
+
+    ST = QT // 2
+
+    def own_part(b):
+        return rows(t * QT + b * ST, ST)
 
     def ag4(i, ref):
-        own_rows = ref.at[own, :]
-        cps = [
-            send(own_rows, own_rows, a4_s.at[i, 0], a4_r.at[i, 0], dsib),
-            send(own_rows, own_rows, a4_s.at[i, 1], a4_r.at[i, 1], dyp),
-        ]
+        st = {}
+
+        def put(b):
+            r = ref.at[own_part(b), :]
+            st["c", b] = send(r, r, a4_s.at[i, b], a4_r.at[i, b], dsib)
+            st["y", b] = send(r, r, a4_s.at[i, 2 + b], a4_r.at[i, 2 + b], dyp)
 
         def fin():
-            cps[1].wait_recv()
-            r = ref.at[rows(yp * QT, QT), :]
-            cps.append(send(r, r, a4_s.at[i, 2], a4_r.at[i, 2], dsib))
-            cps[0].wait_recv()
-            cps[2].wait_recv()
+            for b in range(2):
+                st["y", b].wait_recv()
+                r = ref.at[rows(yp * QT + b * ST, ST), :]
+                st["o", b] = send(r, r, a4_s.at[i, 4 + b], a4_r.at[i, 4 + b], dsib)
+            for b in range(2):
+                st["c", b].wait_recv()
+                st["o", b].wait_recv()
 
         def sent():
-            for cp in cps:
+            for cp in st.values():
                 cp.wait_send()
 
-        return fin, sent
-
-    def rs4(i, part, filler=None):
+        return put, fin, sent
+
+    def rs4(i, part, consume, filler=None):
         r0 = [(1 - y) * HALF, y * HALF]
-        cps = []
+        st = {}
         for k in range(2):
             PB[rows(r0[k], HALF), :] = part(rows(r0[k], HALF)).astype(BF)
-            cps.append(send(PB.at[rows(r0[k] + (1 - c) * QT, QT), :], rsib.at[k], r4_s.at[i, k], r4_r.at[i, k], dsib))
+            for b in range(2):
+                st["c", k, b] = send(
+                    PB.at[rows(r0[k] + (1 - c) * QT + b * ST, ST), :], rsib.at[k, b], r4_s.at[i, 2 * k + b], r4_r.at[i, 2 * k + b], dsib
+                )
             if k == 0:
-                cps[0].wait_recv()
-                mine = rows(r0[0] + c * QT, QT)
-                PB[mine, :] = (PB[mine, :].astype(F32) + rsib[0].astype(F32)).astype(BF)
-                ycp = send(PB.at[mine, :], ry, r4_s.at[i, 2], r4_r.at[i, 2], dyp)
+                for b in range(2):
+                    st["c", 0, b].wait_recv()
+                    mine = rows(r0[0] + c * QT + b * ST, ST)
+                    PB[mine, :] = (PB[mine, :].astype(F32) + rsib[0, b].astype(F32)).astype(BF)
+                    st["y", b] = send(PB.at[mine, :], ry.at[b], r4_s.at[i, 4 + b], r4_r.at[i, 4 + b], dyp)
         if filler is not None:
             filler()
-        cps[1].wait_recv()
-        ycp.wait_recv()
-        total = PB[own, :].astype(F32) + rsib[1].astype(F32) + ry[...].astype(F32)
-        cps[0].wait_send()
-        cps[1].wait_send()
-        ycp.wait_send()
-        return total
+        for b in range(2):
+            st["c", 1, b].wait_recv()
+            st["y", b].wait_recv()
+            consume(b, PB[own_part(b), :].astype(F32) + rsib[1, b].astype(F32) + ry[b].astype(F32))
+        for cp in st.values():
+            cp.wait_send()
 
     def xgather(l):
         st = {}
 
-        def src_rows(j, q):
-            return XA.at[l, rows(zm[j] * TL + q * QT, QT), :]
+        def src_rows(k, q):
+            return XA.at[l, rows(k * TL + q * QT, QT), :]
+
+        def along(k, to, kind):
+            r = src_rows(k, t)
+            return copy_to(r, r, ax_s.at[l, kind * nz + k], ax_r.at[l, k], (d, to, t))
+
+        def hop(j):
+            right = (z - ck[j] + nz) // nz
+            to = z - 1 + 2 * right
+            return (to >= 0) & (to < nz), along(ck[j], to, 0)
+
+        ends = [(z < nz - 1, along(z, z + 1, 0)), (z > 0, along(z, z - 1, 1))]
+
+        def local(j):
+            r = src_rows(ck[j], t)
+            st["y", j] = send(r, r, ax_s.at[l, 2 * nz + ck[j]], ax_r.at[l, nz + ck[j]], dyp)
+            st["c", j] = send(r, r, ax_s.at[l, 3 * nz + ck[j]], ax_r.at[l, 2 * nz + ck[j]], dsib)
 
         def start():
-            r = src_rows(0, t)
+            for ok, cp in ends:
+                pl.when(ok)(cp.start)
             if l > 0:
-                st["c", 0] = send(r, r, ax_s.at[l, nz], ax_r.at[l, nz], dsib)
-                st["y", 0] = send(r, r, ax_s.at[l, 2 * nz], ax_r.at[l, 2 * nz], dyp)
-            for k in range(1, nz):
-                st["z", k] = send(r, r, ax_s.at[l, k], ax_r.at[l, k], (d, zk[k], t))
-
-        def mid(j):
-            st["z", j].wait_recv()
-            r = src_rows(j, t)
-            st["y", j] = send(r, r, ax_s.at[l, 2 * nz + j], ax_r.at[l, 2 * nz + j], dyp)
-            st["c", j] = send(r, r, ax_s.at[l, nz + j], ax_r.at[l, nz + j], dsib)
+                local(0)
+
+        def arrive(j):
+            along(ck[j], z, 0).wait_recv()
+            ok, cp = hop(j)
+            pl.when(ok)(cp.start)
+            local(j)
 
         def fwd(j):
             st["y", j].wait_recv()
-            r = src_rows(j, yp)
-            st["c2", j] = send(r, r, ax_s.at[l, 3 * nz + j], ax_r.at[l, 3 * nz + j], dsib)
+            r = src_rows(ck[j], yp)
+            st["c2", j] = send(r, r, ax_s.at[l, 4 * nz + ck[j]], ax_r.at[l, 3 * nz + ck[j]], dsib)
 
         def fin(j):
             st["c", j].wait_recv()
             st["c2", j].wait_recv()
 
         def sent():
+            for ok, cp in ends + [hop(j) for j in range(1, nz)]:
+                pl.when(ok)(cp.wait_send)
             for cp in st.values():
                 cp.wait_send()
 
-        return start, mid, fwd, fin, sent
+        return start, arrive, fwd, fin, sent
 
     def small(l, r):
         return SV[l, r : r + 1, :]
 
     def kv_proj(l, j):
-        r = rows(zm[j] * TL, TL)
+        r = rows(ck[j] * TL, TL)
         bias = SV[l, 8:9, 0:384]
         KV[l, r, :] = (nn(XA[l, r, :], W[3 * l, :, 0:384]) + bias).astype(BF)
 
@@ -226,7 +297,7 @@
     def masked_scores(l, h, hl, r, j):
         kv = KV[l, r, pl.ds(hl, 128)]
         s = nt(kv, QP[l, :, pl.ds(hl, 128)])
-        sq = segqm[h, pl.ds(pl.multiple_of(zm[j] * nb, nb), nb), :]
+        sq = segqm[h, pl.ds(pl.multiple_of(ck[j] * nb, nb), nb), :]
         sk = segk[r, :]
         parts = []
         for b in range(nb):
@@ -235,7 +306,7 @@
         return kv, jnp.concatenate(parts, axis=0)
 
     def attend(l, j):
-        r = rows(zm[j] * TL, TL)
+        r = rows(ck[j] * TL, TL)
 
         def head(h, carry):
             hl = pl.multiple_of(h * 128, 128)
@@ -274,47 +345,51 @@
         dg = 0.5 * (1.0 + th) + 0.5 * u * (1.0 - th * th) * (k * (1.0 + 3 * 0.044715 * u * u))
         return g, dg
 
-    def forward(l, bg):
-        start, mid, fwd, fin, sent = xg[l]
+    seen = []
+
+    def forward(l, bg, then):
+        start, arrive, fwd, fin, sent = xg[l]
         if l > 0:
             start()
-            mid(1)
+            arrive(1)
             fwd(0)
             fin(0)
+            w_fin(3)
         q_proj(l)
         kv_proj(l, 0)
-        if l > 0:
-            mid(2)
+        arrive(2)
+        fwd(1)
         attend(l, 0)
+        arrive(3)
+        fwd(2)
         bg[0]()
-        if l > 0:
-            mid(3)
-            fwd(1)
         for j in range(1, nz):
             fin(j)
             kv_proj(l, j)
-            if j + 1 < nz:
-                if l > 0:
-                    fwd(j + 1)
             attend(l, j)
-            if j == nz - 2:
-                bg[1]()
+            if j == 1:
+                fwd(3)
+            bg[j]()
         attend_end(l)
         sent()
         wo = W[3 * l, :, 512:768]
-        r = rs4(3 * l, lambda rr: nt(OO[l, rr, :], wo))
-        z1 = XR[...] + r + small(l, 0)
-        n1, rs1 = normalise(z1)
-        N1[l] = n1
-        RS1[l] = rs1
-        h1 = n1 * small(l, 4) + small(l, 1)
-        H1[l, own, :] = h1.astype(BF)
-        XR[...] = h1
-        done, gone = ag4(4 * l, H1.at[l])
-        bg[2]()
+        put, done, gone = ag4(4 * l, H1.at[l])
+
+        def first(b, r):
+            part = pl.ds(b * ST, ST)
+            z1 = XR[part, :] + r + small(l, 0)
+            n1, rs1 = normalise(z1)
+            N1[l, part, :] = n1
+            RS1[l, part, :] = rs1
+            h1 = n1 * small(l, 4) + small(l, 1)
+            H1[l, own_part(b), :] = h1.astype(BF)
+            XR[part, :] = h1
+            put(b)
+
+        rs4(3 * l, lambda rr: nt(OO[l, rr, :], wo), first, bg[4])
+        bg[5]()
         done()
         w_fin(3 * l + 1)
-        w_fin(3 * l + 2)
 
         def ffn(rr):
             u = nn(H1[l, rr, :], W[3 * l + 1]) + small(l, 6)
@@ -322,17 +397,27 @@
             DG[l, rr, :] = dg.astype(BF)
             gb = g.astype(BF)
             G[l, rr, :] = gb
+            if l not in seen:
+                seen.append(l)
+                w_fin(3 * l + 2)
             return nt(gb, W[3 * l + 2])
 
-        r = rs4(3 * l + 1, ffn, gone)
-        bg[3]()
-        z2 = XR[...] + r + small(l, 2)
-        n2, rs2 = normalise(z2)
-        N2[l] = n2
-        RS2[l] = rs2
-        out = n2 * small(l, 5) + small(l, 3)
-        XR[...] = out
-        return out.astype(BF)
+        def fill():
+            gone()
+            bg[6]()
+
+        def second(b, r):
+            part = pl.ds(b * ST, ST)
+            z2 = XR[part, :] + r + small(l, 2)
+            n2, rs2 = normalise(z2)
+            N2[l, part, :] = n2
+            RS2[l, part, :] = rs2
+            out = n2 * small(l, 5) + small(l, 3)
+            XR[part, :] = out
+            then(b, out)
+
+        rs4(3 * l + 1, ffn, second, fill)
+        bg[7]()
 
     gx = {}
     gz = {}
@@ -340,26 +425,28 @@
     if direct:
 
         def g_start(p):
-            ref = W.at[p, rows((1 - d) * (nz * rw), nz * rw), :]
-            gx[p] = send(ref, XRV.at[p], g_s.at[p, 0], g_r.at[p, 0], dx_dev)
+            for k in ck[::-1]:
+                gx[p, len(gx)] = send(
+                    W.at[p, rows(((1 - d) * nz + k) * rw, rw), :], XRV.at[p, rows(k * rw, rw), :], g_s.at[p, k], g_r.at[p, k], dx_dev
+                )
 
         def g_mid(p):
-            gx[p].wait_recv()
-            r = rows(d * (nz * rw), nz * rw)
-            W[p, r, :] = (W[p, r, :].astype(F32) + XRV[p].astype(F32)).astype(BF)
-            gz[p] = [
-                send(W.at[p, rows((d * nz + zk[k]) * rw, rw), :], ZRV.at[p, k - 1], g_s.at[p, k], g_r.at[p, k], (d, zk[k], t))
-                for k in range(1, nz)
-            ]
+            gz[p] = []
+            for k in ck[::-1]:
+                r = rows((d * nz + k) * rw, rw)
+                x = XRV.at[p, rows(k * rw, rw), :]
+                copy_to(x, x, g_s.at[p, k], g_r.at[p, k], dx_dev).wait_recv()
+                W[p, r, :] = (W[p, r, :].astype(F32) + x[...].astype(F32)).astype(BF)
+                if k is not z:
+                    gz[p].append(send(W.at[p, r, :], ZRV.at[p, z], g_s.at[p, nz + k], g_r.at[p, nz + z], (d, k, t)))
 
         def g_fin(p):
-            for cp in gz[p]:
-                cp.wait_recv()
             tot = W[p, rows((d * nz + z) * rw, rw), :].astype(F32)
-            for k in range(nz - 1):
-                tot = tot + ZRV[p, k].astype(F32)
+            for k in ck[1:]:
+                x = ZRV.at[p, k]
+                copy_to(x, x, g_s.at[p, nz + k], g_r.at[p, nz + k], dx_dev).wait_recv()
+                tot = tot + x[...].astype(F32)
             gout[p] = tot
-            pending.append(gx[p])
             pending.extend(gz[p])
     else:
 
@@ -371,17 +458,28 @@
 
         g_fin = g_mid
 
-    def backward(l, bg):
-        dy = DZ[...]
-        n2 = N2[l]
-        SL[l, 3:4, :] = jnp.sum(dy, axis=0, keepdims=True)
-        SL[l, 5:6, :] = jnp.sum(dy * n2, axis=0, keepdims=True)
-        dz2 = norm_back(dy * small(l, 5), n2, RS2[l])
-        SL[l, 2:3, :] = jnp.sum(dz2, axis=0, keepdims=True)
-        DZ[...] = dz2
-        EB[2 * l + 1, own, :] = dz2.astype(BF)
-        done, gone = ag4(4 * l + 2, EB.at[2 * l + 1])
-        bg[0]()
+    def accumulate(l, row, b, v):
+        v = jnp.sum(v, axis=0, keepdims=True)
+        SL[l, row : row + 1, :] = v if b == 0 else SL[l, row : row + 1, :] + v
+
+    def second_back(l):
+        put, done, gone = ag4(4 * l + 2, EB.at[2 * l + 1])
+
+        def one(b, dy):
+            part = pl.ds(b * ST, ST)
+            n2 = N2[l, part, :]
+            accumulate(l, 3, b, dy)
+            accumulate(l, 5, b, dy * n2)
+            dz2 = norm_back(dy * small(l, 5), n2, RS2[l, part, :])
+            accumulate(l, 2, b, dz2)
+            DZ[part, :] = dz2
+            EB[2 * l + 1, own_part(b), :] = dz2.astype(BF)
+            put(b)
+
+        return one, done, gone
+
+    def backward(l, bg, done, gone, then):
+        bg.get(0, nop)()
         done()
 
         def ffn_back(rr):
@@ -399,19 +497,25 @@
             W[3 * l + 1] = tn(H1[l], DU[...]).astype(BF)
             g_start(3 * l + 1)
             SL[l, 6:7, :] = jnp.sum(DU[...].astype(F32), axis=0, keepdims=True)
-
-        r = rs4(3 * l + 2, ffn_back, fill)
-        dh1 = DZ[...] + r
-        n1 = N1[l]
-        SL[l, 1:2, :] = jnp.sum(dh1, axis=0, keepdims=True)
-        SL[l, 4:5, :] = jnp.sum(dh1 * n1, axis=0, keepdims=True)
-        dz1 = norm_back(dh1 * small(l, 4), n1, RS1[l])
-        SL[l, 0:1, :] = jnp.sum(dz1, axis=0, keepdims=True)
-        DZ[...] = dz1
-        EB[2 * l, own, :] = dz1.astype(BF)
-        done, gone1 = ag4(4 * l + 3, EB.at[2 * l])
-        bg[1]()
-        done()
+            bg.get(1, nop)()
+
+        put, done1, gone1 = ag4(4 * l + 3, EB.at[2 * l])
+
+        def first_back(b, r):
+            part = pl.ds(b * ST, ST)
+            dh1 = DZ[part, :] + r
+            n1 = N1[l, part, :]
+            dz1 = norm_back(dh1 * small(l, 4), n1, RS1[l, part, :])
+            DZ[part, :] = dz1
+            EB[2 * l, own_part(b), :] = dz1.astype(BF)
+            put(b)
+            accumulate(l, 1, b, dh1)
+            accumulate(l, 4, b, dh1 * n1)
+            accumulate(l, 0, b, dz1)
+
+        rs4(3 * l + 2, ffn_back, first_back, fill)
+        bg.get(2, nop)()
+        done1()
         doo = nn(EB[2 * l], W[3 * l, :, 512:768]).astype(BF).astype(F32)
         lo = low_lanes((TL, 128))
         da, db = doo[:, 0:128], doo[:, 128:256]
@@ -424,10 +528,10 @@
         DEL[2] = jnp.sum(prod[64:128], axis=0, keepdims=True)
 
         xs = {}
-        order = list(range(1, nz)) + [0]
+        order = list(range(nz - 1, 0, -1)) + [0]
 
         def attend_back(j, first):
-            r = rows(zm[j] * TL, TL)
+            r = rows(ck[j] * TL, TL)
 
             def head(h, carry):
                 hl = pl.multiple_of(h * 128, 128)
@@ -450,7 +554,7 @@
         def dx_parts(j):
             for k in range(2):
                 r0 = [(1 - y) * HALF, y * HALF][k]
-                v = nt(DKV[rows(zm[j] * TL + r0, HALF), :], W[3 * l, :, 0:384])
+                v = nt(DKV[rows(ck[j] * TL + r0, HALF), :], W[3 * l, :, 0:384])
                 if j == 0:
                     v = v + nt(DQ[rows(r0, HALF), :], W[3 * l, :, 384:640])
                 DXP[j, rows(r0, HALF), :] = v.astype(BF)
@@ -469,14 +573,14 @@
             if j == 0:
                 return tot
             DXP[j, own, :] = tot.astype(BF)
-            xs["z", j] = send(DXP.at[j, own, :], xz.at[l, j - 1], r16_s.at[l, 3 * nz + j - 1], r16_r.at[l, 3 * nz + j - 1], (d, zm[j], t))
+            xs["z", j] = send(DXP.at[j, own, :], xz.at[l, z], r16_s.at[l, 3 * nz + ck[j]], r16_r.at[l, 3 * nz + z], (d, ck[j], t))
 
         for i, j in enumerate(order):
             attend_back(j, i == 0)
             if i >= 2:
                 dx_z(order[i - 2])
-            if i == 1:
-                bg[2]()
+            if i < 2:
+                bg.get(3 + i, nop)()
             if j == 0:
                 a01 = ACC[0]
                 hi = lax.broadcasted_iota(jnp.int32, a01.shape, 0) < 64
@@ -484,44 +588,56 @@
                 DQ[:, 128:256] = (jnp.where(hi, ACC[2], 0.0).T * 0.125).astype(BF)
             dx_parts(j)
             dx_y(j)
-        dx_z(order[nz - 2])
         gone1()
         w_sent(3 * l)
         xown = XA[l, rows(z * TL, TL), :]
         gq = tn(xown, DQ[...])
         go = tn(EB[2 * l], OO[l])
         gkv = tn(XA[l], DKV[...])
-        mine_total = dx_z(0)
+        SL[l, 7:8, 0:384] = jnp.sum(DKV[...].astype(F32), axis=0, keepdims=True)
+        SL[l, 7:8, 384:640] = jnp.sum(DQ[...].astype(F32), axis=0, keepdims=True)
+        SL[l, 7:8, 640:768] = jnp.zeros((1, 128), F32)
         W[3 * l, :, 0:384] = gkv.astype(BF)
         W[3 * l, :, 384:512] = gq[:, 0:128].astype(BF)
         W[3 * l, :, 512:640] = (gq[:, 128:256] + go[:, 0:128]).astype(BF)
         W[3 * l, :, 640:768] = go[:, 128:256].astype(BF)
         g_start(3 * l)
-        SL[l, 7:8, 0:384] = jnp.sum(DKV[...].astype(F32), axis=0, keepdims=True)
-        SL[l, 7:8, 384:640] = jnp.sum(DQ[...].astype(F32), axis=0, keepdims=True)
-        SL[l, 7:8, 640:768] = jnp.zeros((1, 128), F32)
-        tot = DZ[...] + mine_total
-        for j in range(1, nz):
-            xs["z", j].wait_recv()
-            tot = tot + xz[l, j - 1].astype(F32)
-        DZ[...] = tot
+        dx_z(order[nz - 2])
+        bg.get(5, nop)()
+        tot = DZ[...] + dx_z(0)
+        for k in ck[1:]:
+            x = xz.at[l, k]
+            copy_to(x, x, r16_s.at[l, 3 * nz + k], r16_r.at[l, 3 * nz + k], dsib).wait_recv()
+            tot = tot + x[...].astype(F32)
+        then(tot)
         for cp in xs.values():
             cp.wait_send()
-        return tot
 
     xg = [xgather(0), xgather(1)]
+
+    def run(*steps):
+        def go():
+            for fn, *a in steps:
+                fn(*a)
+
+        return go
+
+    nop = run()
+    for p in (6, 0, 1, 2):
+        w_o(p)
+    w_a(6)
+    w_a(0)
     XA[0, rows(z * TL, TL), :] = xin[...]
     XR[...] = xin[own, :].astype(F32)
-    w_z(6)
+    w_b(6)
+    w_b(0)
+    w_c(6)
+    w_c(0)
     xg[0][0]()
-    w_z(0)
-    for j in range(1, nz):
-        xg[0][1](j)
-    w_x(6)
-    w_x(0)
-    w_z(1)
-    for j in range(1, nz):
-        xg[0][2](j)
+    w_d(6)
+    w_d(0)
+    for p in (3, 4, 5):
+        w_o(p)
     w_fin(6)
     if direct:
         wide = DM - 128
@@ -541,79 +657,82 @@
             SV[l, 0:8, :] = acc[0:8]
             SV[l, 7:8, :] = bq
             SV[l, 8:9, :] = kvb
+    xg[0][1](1)
     w_fin(0)
-
-    def after_first():
-        w_x(1)
-        w_z(2)
-
-    def b2():
-        w_x(2)
-        w_z(3)
-
-    def b3():
-        pass
-
-    def b4():
-        w_x(3)
-        w_z(4)
-
-    x1 = forward(0, [after_first, b2, b3, b4])
-    XA[1, rows(z * TL + t * QT, QT), :] = x1
-    w_fin(3)
-
-    def c1():
-        w_x(4)
-        w_z(5)
-
-    def c2():
-        w_x(5)
-
-    nop = lambda: None
-    x2 = forward(1, [c1, c2, nop, nop])
-    EB[0, own, :] = x2
-    act_done, act_sent = ag4(1, EB.at[0])
-    DZ[...] = cot[own, :].astype(F32)
+    def next_input(b, v):
+        XA[1, rows(z * TL + t * QT + b * ST, ST), :] = v.astype(BF)
+
+    forward(0, [
+        run((w_a, 1)),
+        nop,
+        run((w_b, 1)),
+        run((w_a, 2), (w_c, 1)),
+        run((w_d, 1), (w_b, 2)),
+        run((w_c, 2), (w_d, 2), (w_a, 3)),
+        run((w_b, 3), (w_c, 3)),
+        run((w_d, 3), (w_a, 4)),
+    ], next_input)
+    start_back, done, gone = second_back(1)
+
+    def last_output(b, v):
+        start_back(b, cot[own_part(b), :].astype(F32))
+        EB[0, own_part(b), :] = v.astype(BF)
+
+    forward(1, [
+        run((w_b, 4)),
+        run((w_c, 4)),
+        run((w_d, 4)),
+        run((w_a, 5)),
+        run((w_b, 5)),
+        run((w_c, 5), (w_d, 5)),
+        nop,
+        nop,
+    ], last_output)
+    act_put, act_done, act_sent = ag4(1, EB.at[0])
+
+    def act_start():
+        act_put(0)
+        act_put(1)
 
     def act_end():
         act_done()
         act[...] = EB[0]
         act_sent()
 
-    def m5():
-        g_mid(5)
-
-    def m4():
-        g_mid(4)
-
-    backward(1, [act_end, m5, m4])
-
-    def m3():
-        g_mid(3)
-        g_fin(5)
-
-    def m2():
-        g_mid(2)
-        g_fin(4)
-
-    def m1():
-        g_mid(1)
-        g_fin(3)
-
-    dx = backward(0, [m3, m2, m1])
-    EB[3, own, :] = dx.astype(BF)
-    dx_done, dx_sent = ag4(5, EB.at[3])
-
-    cps = [send(SL, St1, s_s.at[0], s_r.at[0], dsib)]
-    cps[0].wait_recv()
-    cps[0].wait_send()
+    lower = second_back(0)
+
+    def to_lower(dy):
+        for b in range(2):
+            lower[0](b, dy[b * ST : (b + 1) * ST])
+
+    backward(1, {0: run((act_start,)), 1: run((act_end,)), 3: run((g_mid, 5)), 5: run((g_mid, 4))}, done, gone, to_lower)
+
     keep = lax.broadcasted_iota(jnp.int32, SL.shape, 1) < 6
-    SL[...] = SL[...] + jnp.where(keep, St1[...], 0.0)
-    cps.append(send(SL, St2, s_s.at[1], s_r.at[1], dyp))
-    cps[1].wait_recv()
-    cps[1].wait_send()
+
+    def s1():
+        cp = send(SL, St1, s_s.at[0], s_r.at[0], dsib)
+        cp.wait_recv()
+        cp.wait_send()
+        SL[...] = SL[...] + jnp.where(keep, St1[...], 0.0)
+        sc.append(send(SL, St2, s_s.at[1], s_r.at[1], dyp))
+
+    sc = []
+    dx_put, dx_done, dx_sent = ag4(5, EB.at[3])
+
+    def to_output(dx):
+        EB[3, own, :] = dx.astype(BF)
+        dx_put(0)
+        dx_put(1)
+
+    backward(
+        0, {1: run((g_mid, 3), (g_fin, 5)), 3: run((g_mid, 2), (g_fin, 4)), 5: run((s1,), (g_mid, 1), (g_fin, 3))}, lower[1], lower[2], to_output
+    )
+
+    sc[0].wait_recv()
+    sc[0].wait_send()
     SL[...] = SL[...] + jnp.where(keep, St2[...], 0.0)
     zc = [send(SL, Sz.at[k - 1], s_s.at[1 + k], s_r.at[1 + k], (d, zk[k], t)) for k in range(1, nz)]
+    g_mid(0)
     for cp in zc:
         cp.wait_recv()
     for cp in zc:
@@ -621,22 +740,22 @@
     tot = SL[...]
     for k in range(nz - 1):
         tot = tot + Sz[k]
-    g_mid(0)
     if direct:
         SL[...] = tot
         xc = send(SL, Sx, s_s.at[1 + nz], s_r.at[1 + nz], dx_dev)
+    dx_done()
+    dxo[...] = EB[3]
+    dx_sent()
+    g_fin(2)
+    g_fin(1)
+    if direct:
         xc.wait_recv()
         xc.wait_send()
         tot = tot + Sx[...]
     gsm[...] = tot
-    g_fin(2)
-    g_fin(1)
-    dx_done()
-    dxo[...] = EB[3]
-    dx_sent()
     g_fin(0)
     w_sent(6)
-    for cp in pending:
+    for cp in pending + list(gx.values()):
         cp.wait_send()
 
 
@@ -717,12 +836,12 @@
         pltpu.VMEM((QT, DM), F32),
         pltpu.VMEM((2 * L, TL, DM), BF),
         pltpu.VMEM((TL, DM), BF),
-        pltpu.VMEM((2, QT, DM), BF),
-        pltpu.VMEM((QT, DM), BF),
+        pltpu.VMEM((2, 2, QT // 2, DM), BF),
+        pltpu.VMEM((2, QT // 2, DM), BF),
         pltpu.VMEM((nz, TL, DM), BF),
         pltpu.VMEM((nz, 2, QT, DM), BF),
         pltpu.VMEM((nz, QT, DM), BF),
-        pltpu.VMEM((L, nz - 1, QT, DM), BF),
+        pltpu.VMEM((L, nz, QT, DM), BF),
         pltpu.VMEM((3, 128, TL), F32),
         pltpu.VMEM((3, 1, TL), F32),
         pltpu.VMEM((3, 1, TL), F32),
@@ -732,18 +851,18 @@
         pltpu.VMEM((TL, 384), BF),
         pltpu.VMEM((3, 1, TL), F32),
         pltpu.VMEM((3 * L, xr, DM) if direct else (1, 16, 128), BF),
-        pltpu.VMEM((3 * L, nz - 1, rw, DM) if direct else (1, 1, 16, 128), BF),
+        pltpu.VMEM((3 * L, nz, rw, DM) if direct else (1, 1, 16, 128), BF),
         pltpu.VMEM((L, 8, DM), F32),
         pltpu.VMEM((L, 8, DM), F32),
         pltpu.VMEM((L, 8, DM), F32),
         pltpu.VMEM((nz - 1, L, 8, DM), F32),
         pltpu.VMEM((L, 8, DM), F32),
-        dma((7, nz)), dma((7, nz)),
+        dma((7, 5 + nz)), dma((7, 2 * nz)),
+        dma((L, 5 * nz)), dma((L, 4 * nz)),
+        dma((8, 6)), dma((8, 6)),
+        dma((6, 6)), dma((6, 6)),
         dma((L, 4 * nz)), dma((L, 4 * nz)),
-        dma((8, 3)), dma((8, 3)),
-        dma((6, 3)), dma((6, 3)),
-        dma((L, 4 * nz)), dma((L, 4 * nz)),
-        dma((6, nz)), dma((6, nz)),
+        dma((6, 2 * nz)), dma((6, 2 * nz)),
         dma((2 + nz,)), dma((2 + nz,)),
     ]
     act, dx, gout, gsm = pl.pallas_call(

time: 359 us -> 316 us (0.88)
  Pallas kernels: 332 us -> 289 us
    pallas_call x1, Pallas kernels: 332 us -> 289 us  [shards(): pl.pallas_call(functools.partial(body, direct, nz, rw), out_shape=(jax.Sh...]
where the time goes in v2:
time: 316 us; the launch traced here: 312 us
  Pallas kernels  289 us (91%)
  local copies, waits for them, and re-layouts  19.2 us (6%)
  other arithmetic  3.21 us (1%)
    pallas_call x1, Pallas kernels, shards(): pl.pallas_call(functools.partial(body, direct, nz, rw), out_shape=(jax.Sh...  289 us

profile of v2, /device:TPU:0, one launch (start us, length us, event | category | flops | bytes accessed | tf_op | source)
XLA Modules:
  0.0 312.4 jit_solution(10190181946751970812)
XLA Ops:
  0.6 0.0 copy-start
  0.7 0.0 copy-start.5
  0.7 1.2 fusion.7
  1.9 0.0 copy-start.3
  1.9 0.1 copy.109
  2.0 0.1 copy.110
  2.1 0.1 copy.117
  2.3 0.1 copy.119
  2.4 0.0 copy-start.4
  2.4 0.1 copy.120
  2.5 0.1 copy.111
  2.6 0.1 copy.112
  2.8 0.1 copy.113
  2.9 0.1 copy.114
  3.0 0.1 copy.115
  3.1 0.1 copy.116
  3.2 0.1 copy.118
  3.3 0.0 copy-done.5
  3.4 0.1 copy.121
  3.5 0.1 copy.122
  3.6 0.1 copy.123
  3.7 0.2 concatenate.23
  4.0 0.0 copy-done.3
  4.0 0.0 copy-done.4
  4.1 0.0 copy-start.6
  4.1 0.0 copy-start.9
  4.1 0.0 copy-start.8
  4.1 0.0 copy-start.7
  4.1 0.0 copy-start.10
  4.1 0.1 pad_maximum_fusion
  4.2 1.0 copy.96
  5.2 0.0 copy-done
  5.2 0.1 constant_dynamic-slice_fusion.4
  5.3 0.1 fusion
  5.4 0.1 fusion.2
  5.5 0.1 copy.97
  5.6 0.2 broadcast_in_dim.52
  5.8 0.2 broadcast_in_dim.53
  6.0 0.0 copy-done.6
  6.0 0.7 broadcast_select_fusion.segqm
  6.7 0.0 copy-done.9
  6.7 0.0 copy-done.8
  6.8 0.0 copy-done.7
  6.8 0.0 copy-done.10
  6.9 1.2 concatenate.24.sm
  8.1 1.3 broadcast_in_dim.51.segk
  9.4 288.6 %encoder.1 = (bf16[512,768]{1,0:T(8,128)(2,1)}, bf16[512,768]{1,0:T(8,128)(2,1)}, f32[6,96,768]{2,1,0:T(8,128)}, f32[2,8,768]{2,1,0:T(8,128)}) custom-call(bf16[6,96,768]{2,1,0:T(8,128)(2,1)} %bitcast.71, f32[2,16,128]{2,1,0:T(8,128)} %concatenate.24.sm, bf16[512,768]{1,0:T(8,128)(2,1)} %bitcast.77, bf16[512,768]{1,0:T(8,128)(2,1)} %bitcast.78, ...), custom_call_target="tpu_custom_call" | custom-call | tf_op jit(solution)/shard_map/encoder/pallas_call | solution.py:868
  298.0 0.8 slice.145
  298.8 0.8 slice.146
  299.6 0.8 copy.101
  300.4 0.1 fusion.4
  300.5 0.6 copy.104
  301.1 2.6 slice_bitcast_fusion
  303.7 0.3 copy.124
  304.0 0.7 maximum_bitcast_fusion.2
  304.7 0.0 copy-start.2
  304.8 0.0 copy-start.1
  304.8 1.1 copy.103
  305.9 1.4 constant_dynamic-slice_fusion
  307.3 1.4 constant_dynamic-slice_fusion.2
  308.7 1.4 constant_dynamic-slice_fusion.1
  310.0 1.3 bitcast_convert_fusion
  311.3 0.0 copy-done.1
  311.3 0.9 copy.132
  (31 shorter events, 0.3 us)
Async XLA Ops:
  0.6 4.6 %copy-start = (s32[1,3,32,3]{2,0,3,1:T(1,128)S(1)}, s32[1,3,32,3]{2,0,3,1:T(1,128)}, u32[]{:S(2)}) copy-start(s32[1,3,32,3]{2,0,3,1:T(1,128)} %param.15) | copy-start | bytes 3460
  0.7 2.7 copy-start.5
  1.9 2.1 copy-start.3
  2.4 1.6 copy-start.4
  4.1 1.9 copy-start.6
  4.1 2.6 copy-start.9
  4.1 2.7 copy-start.8
  4.1 2.7 copy-start.7
  4.1 2.7 copy-start.10
  304.7 5.3 %copy-start.2 = (bf16[512,768]{1,0:T(8,128)(2,1)S(1)}, bf16[512,768]{1,0:T(8,128)(2,1)}, u32[]{:S(2)}) copy-start(bf16[512,768]{1,0:T(8,128)(2,1)} %get-tuple-element.15) | copy-start | bytes 2359300
  304.8 6.5 %copy-start.1 = (bf16[512,768]{1,0:T(8,128)(2,1)S(1)}, bf16[512,768]{1,0:T(8,128)(2,1)}, u32[]{:S(2)}) copy-start(bf16[512,768]{1,0:T(8,128)(2,1)} %get-tuple-element.14) | copy-start | bytes 2359300

commit v3 on v2

--- a/solution.py
+++ b/solution.py
@@ -44,13 +44,25 @@
 
 
 def body(
-    direct, nz, rw,
-    wl, sm, xin, cot, segk, segqm,
-    act, dxo, gout, gsm,
+    direct, nz, rw, n_in, *refs
+):
+    ins, refs = refs[:n_in], refs[n_in:]
+    if direct:
+        wl, xin, cot, seg, rnd, sh_in, ga_in, mb_in, qv_in = ins
+        act, dxo, gq_out, go_out, g1_out, g2_out, gsm = refs[:7]
+        refs = refs[7:]
+    else:
+        wl, xin, cot, seg, rnd, sm = ins
+        act, dxo, gout, gsm = refs[:4]
+        refs = refs[4:]
+    (
     W, SG, SV, XA, KV, QP, OO, LSE, H1, DG, G, N1, N2, RS1, RS2, XR, DZ, EB,
     PB, rsib, ry, DXP, xsib, xy, xz, ACC, MX, LS, DKV, DU, DQ, DO, DEL, XRV, ZRV, SL, St1, St2, Sz, Sx,
-    wg_s, wg_r, ax_s, ax_r, a4_s, a4_r, r4_s, r4_r, r16_s, r16_r, g_s, g_r, s_s, s_r,
-):
+        SMS, segk, segqm, SA,
+        wg_s, wg_r, ax_s, ax_r, a4_s, a4_r, r4_s, r4_r, r16_s, r16_r, g_s, g_r, s_s, s_r,
+    ) = refs
+    if direct:
+        sm = SMS
     d, z, t = lax.axis_index("dp"), lax.axis_index("seq"), lax.axis_index("tensor")
     c = t % 2
     y = t // 2
@@ -65,7 +77,6 @@
     edge = (1 - z) * (1 - upper) + (z - 2) * upper
     inner = 1 - edge
     ck = [z] + [o + upper * (nz - 1 - 2 * o) for o in (edge, 2, 3)]
-    pending = []
 
     bar = pltpu.get_barrier_semaphore()
     peers = [dsib, dyp] + [(d, zk[k], t) for k in range(1, nz)]
@@ -420,7 +431,6 @@
         bg[7]()
 
     gx = {}
-    gz = {}
 
     if direct:
 
@@ -430,24 +440,67 @@
                     W.at[p, rows(((1 - d) * nz + k) * rw, rw), :], XRV.at[p, rows(k * rw, rw), :], g_s.at[p, k], g_r.at[p, k], dx_dev
                 )
 
+        def g_slot(p, k):
+            return W.at[p, rows((d * nz + k) * rw, rw), :]
+
+        def g_to(p, part, to, slot_there):
+            return copy_to(g_slot(p, part), ZRV.at[p, slot_there], g_s.at[p, nz + part], g_r.at[p, nz + slot_there], (d, to, t))
+
+        def g_landed(p, k):
+            x = ZRV.at[p, k]
+            copy_to(x, x, g_s.at[p, nz + k], g_r.at[p, nz + k], dx_dev).wait_recv()
+
+        def g_far(p):
+            return lambda: g_to(p, ck[3], ck[1], ck[1]), lambda: g_to(p, ck[3], ck[3], z)
+
         def g_mid(p):
-            gz[p] = []
             for k in ck[::-1]:
-                r = rows((d * nz + k) * rw, rw)
+                r = g_slot(p, k)
                 x = XRV.at[p, rows(k * rw, rw), :]
                 copy_to(x, x, g_s.at[p, k], g_r.at[p, k], dx_dev).wait_recv()
-                W[p, r, :] = (W[p, r, :].astype(F32) + x[...].astype(F32)).astype(BF)
-                if k is not z:
-                    gz[p].append(send(W.at[p, r, :], ZRV.at[p, z], g_s.at[p, nz + k], g_r.at[p, nz + z], (d, k, t)))
+                r[...] = (r[...].astype(F32) + x[...].astype(F32)).astype(BF)
+                if k is ck[3]:
+                    pl.when(edge == 1)(g_far(p)[0]().start)
+                elif k is not z:
+                    g_to(p, k, k, z).start()
+
+        def g_add(p):
+            @pl.when(inner == 1)
+            def _():
+                g_landed(p, z)
+                r = g_slot(p, ck[3])
+                r[...] = (r[...].astype(F32) + ZRV[p, z].astype(F32)).astype(BF)
+                g_far(p)[1]().start()
 
         def g_fin(p):
-            tot = W[p, rows((d * nz + z) * rw, rw), :].astype(F32)
-            for k in ck[1:]:
-                x = ZRV.at[p, k]
-                copy_to(x, x, g_s.at[p, nz + k], g_r.at[p, nz + k], dx_dev).wait_recv()
-                tot = tot + x[...].astype(F32)
-            gout[p] = tot
-            pending.extend(gz[p])
+            l = p // 3
+            goal = (SA, g1_out.at[l], g2_out.at[l])[p % 3]
+            tot = g_slot(p, z)[...].astype(F32)
+            for k in ck[1:3]:
+                g_landed(p, k)
+                tot = tot + ZRV[p, k].astype(F32)
+            goal[...] = tot
+
+            @pl.when(inner == 1)
+            def _():
+                g_landed(p, ck[3])
+                goal[...] = goal[...] + ZRV[p, ck[3]].astype(F32)
+                g_far(p)[1]().wait_send()
+
+            pl.when(edge == 1)(g_far(p)[0]().wait_send)
+            for k in ck[1:3]:
+                g_to(p, k, k, z).wait_send()
+            if p % 3 == 0:
+                tile = [SA[:, 128 * i : 128 * (i + 1)] for i in range(6)]
+                lo = low_lanes(tile[0].shape)
+                gq_out[l, 0, :, 0:128] = tile[3]
+                gq_out[l, 0, :, 128:192] = tile[4][:, 0:64]
+                gq_out[l, 1, :, 0:128] = jnp.where(lo, tile[0], tile[1])
+                gq_out[l, 1, :, 128:192] = tile[2][:, 0:64]
+                gq_out[l, 2, :, 0:128] = pltpu.roll(jnp.where(lo, tile[1], tile[0]), 64, 1)
+                gq_out[l, 2, :, 128:192] = pltpu.roll(tile[2], 64, 1)[:, 0:64]
+                go_out[l, :, 0:128] = pltpu.roll(tile[5], 64, 1)
+                go_out[l, :, 128:192] = pltpu.roll(tile[4], 64, 1)[:, 0:64]
     else:
 
         def g_start(p):
@@ -456,7 +509,7 @@
         def g_mid(p):
             pass
 
-        g_fin = g_mid
+        g_add = g_fin = g_mid
 
     def accumulate(l, row, b, v):
         v = jnp.sum(v, axis=0, keepdims=True)
@@ -573,7 +626,28 @@
             if j == 0:
                 return tot
             DXP[j, own, :] = tot.astype(BF)
-            xs["z", j] = send(DXP.at[j, own, :], xz.at[l, z], r16_s.at[l, 3 * nz + ck[j]], r16_r.at[l, 3 * nz + z], (d, ck[j], t))
+            if j == nz - 1:
+                pl.when(edge == 1)(dx_far()[0]().start)
+            else:
+                dx_to(j, ck[j], z).start()
+
+        def dx_to(j, to, there):
+            return copy_to(DXP.at[j, own, :], xz.at[l, there], r16_s.at[l, 3 * nz + ck[j]], r16_r.at[l, 3 * nz + there], (d, to, t))
+
+        def dx_far():
+            return lambda: dx_to(nz - 1, ck[1], ck[1]), lambda: dx_to(nz - 1, ck[nz - 1], z)
+
+        def dx_landed(k):
+            x = xz.at[l, k]
+            copy_to(x, x, r16_s.at[l, 3 * nz + k], r16_r.at[l, 3 * nz + k], dsib).wait_recv()
+
+        def dx_add():
+            @pl.when(inner == 1)
+            def _():
+                dx_landed(z)
+                j = nz - 1
+                DXP[j, own, :] = (DXP[j, own, :].astype(F32) + xz[l, z].astype(F32)).astype(BF)
+                dx_far()[1]().start()
 
         for i, j in enumerate(order):
             attend_back(j, i == 0)
@@ -603,17 +677,47 @@
         W[3 * l, :, 640:768] = go[:, 128:256].astype(BF)
         g_start(3 * l)
         dx_z(order[nz - 2])
+        dx_add()
         bg.get(5, nop)()
-        tot = DZ[...] + dx_z(0)
-        for k in ck[1:]:
-            x = xz.at[l, k]
-            copy_to(x, x, r16_s.at[l, 3 * nz + k], r16_r.at[l, 3 * nz + k], dsib).wait_recv()
-            tot = tot + x[...].astype(F32)
-        then(tot)
+        DZ[...] = DZ[...] + dx_z(0)
+        for k in ck[1:3]:
+            dx_landed(k)
+            DZ[...] = DZ[...] + xz[l, k].astype(F32)
+
+        @pl.when(inner == 1)
+        def _():
+            dx_landed(ck[3])
+            DZ[...] = DZ[...] + xz[l, ck[3]].astype(F32)
+            dx_far()[1]().wait_send()
+
+        then(DZ[...])
+        pl.when(edge == 1)(dx_far()[0]().wait_send)
+        for j in (1, 2):
+            dx_to(j, ck[j], z).wait_send()
         for cp in xs.values():
             cp.wait_send()
 
     xg = [xgather(0), xgather(1)]
+
+    def masks():
+        length = seg.shape[1]
+        nblk = length // BLK
+        for i in range(length // 128):
+            row = seg[:, 128 * i : 128 * (i + 1)].astype(F32)
+            segk[128 * i : 128 * (i + 1), :] = jnp.broadcast_to(row, (128, 128)).T
+        segq = seg[:, pl.ds(pl.multiple_of(z * TL, TL), TL)].astype(F32)
+        block = lax.broadcasted_iota(jnp.int32, (1, TL), 1) // BLK
+        key = lax.broadcasted_iota(jnp.int32, (nblk, TL), 0)
+        away = key - (z * nb + lax.broadcasted_iota(jnp.int32, (nblk, TL), 1) // BLK)
+        near = (away >= -1) & (away <= 1) | (key == 0) | (key == nblk - 1)
+        for h in range(3):
+            ok = near
+            for r in range(rnd.shape[2]):
+                pick = jnp.zeros((1, TL), jnp.int32)
+                for b in range(nb):
+                    pick = jnp.where(block == b, rnd[h, z * nb + b, r], pick)
+                ok = ok | (key == pick)
+            segqm[h] = jnp.where(ok, segq, -1.0)
 
     def run(*steps):
         def go():
@@ -623,6 +727,13 @@
         return go
 
     nop = run()
+    if direct:
+        SMS[...] = jnp.zeros_like(SMS)
+        for l in range(LAYERS):
+            SMS[l, 0:4, 0:rw] = sh_in[l].astype(BF).astype(F32)
+            SMS[l, 4:6, 0:rw] = ga_in[l].astype(BF).astype(F32)
+            SMS[l, 6:7, 0:rw] = mb_in[l].astype(BF).astype(F32)
+            SMS[l, 8:10, 0 : rw // 4] = qv_in[l].astype(BF).astype(F32)
     for p in (6, 0, 1, 2):
         w_o(p)
     w_a(6)
@@ -634,6 +745,7 @@
     w_c(6)
     w_c(0)
     xg[0][0]()
+    masks()
     w_d(6)
     w_d(0)
     for p in (3, 4, 5):
@@ -664,13 +776,13 @@
 
     forward(0, [
         run((w_a, 1)),
-        nop,
+        run(),
         run((w_b, 1)),
         run((w_a, 2), (w_c, 1)),
-        run((w_d, 1), (w_b, 2)),
-        run((w_c, 2), (w_d, 2), (w_a, 3)),
-        run((w_b, 3), (w_c, 3)),
-        run((w_d, 3), (w_a, 4)),
+        run((w_d, 1), (w_b, 2), (w_a, 3)),
+        run((w_c, 2), (w_d, 2)),
+        run((w_b, 3), (w_a, 4), (w_c, 3)),
+        run((w_d, 3)),
     ], next_input)
     start_back, done, gone = second_back(1)
 
@@ -679,14 +791,14 @@
         EB[0, own_part(b), :] = v.astype(BF)
 
     forward(1, [
-        run((w_b, 4)),
+        run((w_b, 4), (w_a, 5)),
         run((w_c, 4)),
         run((w_d, 4)),
-        run((w_a, 5)),
+        run(),
         run((w_b, 5)),
         run((w_c, 5), (w_d, 5)),
-        nop,
-        nop,
+        run(),
+        run(),
     ], last_output)
     act_put, act_done, act_sent = ag4(1, EB.at[0])
 
@@ -705,7 +817,7 @@
         for b in range(2):
             lower[0](b, dy[b * ST : (b + 1) * ST])
 
-    backward(1, {0: run((act_start,)), 1: run((act_end,)), 3: run((g_mid, 5)), 5: run((g_mid, 4))}, done, gone, to_lower)
+    backward(1, {0: run((act_start,)), 1: run((act_end,)), 3: run((g_mid, 5)), 4: run((g_add, 5)), 5: run((g_mid, 4))}, done, gone, to_lower)
 
     keep = lax.broadcasted_iota(jnp.int32, SL.shape, 1) < 6
 
@@ -725,13 +837,14 @@
         dx_put(1)
 
     backward(
-        0, {1: run((g_mid, 3), (g_fin, 5)), 3: run((g_mid, 2), (g_fin, 4)), 5: run((s1,), (g_mid, 1), (g_fin, 3))}, lower[1], lower[2], to_output
+        0, {1: run((g_add, 4), (g_mid, 3), (g_fin, 5)), 3: run((g_add, 3), (g_mid, 2), (g_fin, 4)), 4: run((g_add, 2)), 5: run((s1,), (g_mid, 1), (g_fin, 3))}, lower[1], lower[2], to_output
     )
 
     sc[0].wait_recv()
     sc[0].wait_send()
     SL[...] = SL[...] + jnp.where(keep, St2[...], 0.0)
     zc = [send(SL, Sz.at[k - 1], s_s.at[1 + k], s_r.at[1 + k], (d, zk[k], t)) for k in range(1, nz)]
+    g_add(1)
     g_mid(0)
     for cp in zc:
         cp.wait_recv()
@@ -743,8 +856,9 @@
     if direct:
         SL[...] = tot
         xc = send(SL, Sx, s_s.at[1 + nz], s_r.at[1 + nz], dx_dev)
+    g_add(0)
     dx_done()
-    dxo[...] = EB[3]
+    dxo[...] = EB[3].astype(F32)
     dx_sent()
     g_fin(2)
     g_fin(1)
@@ -752,10 +866,21 @@
         xc.wait_recv()
         xc.wait_send()
         tot = tot + Sx[...]
-    gsm[...] = tot
+    if direct:
+        lane = lax.broadcasted_iota(jnp.int32, (8, DM), 1)
+        for l in range(LAYERS):
+            x = tot[l]
+            gsm[l, 0:8, :] = pltpu.roll(x, lax.rem(DM - slot * rw, DM), 1)[:, 0:128]
+            gq = pltpu.roll(x, DM - 384, 1)
+            gv = jnp.where(lane < 128, pltpu.roll(x, DM - 64, 1), pltpu.roll(x, DM - 192, 1))
+            back = lax.rem(DM - slot * (rw // 4), DM)
+            gsm[l, 8:16, :] = pltpu.roll(gq, back, 1)[:, 0:128]
+            gsm[l, 16:24, :] = pltpu.roll(gv, back, 1)[:, 0:128]
+    else:
+        gsm[...] = tot
     g_fin(0)
     w_sent(6)
-    for cp in pending + list(gx.values()):
+    for cp in list(gx.values()):
         cp.wait_send()
 
 
@@ -779,11 +904,7 @@
         return v.astype(BF).astype(F32)
 
     if direct:
-        def lanes(v):
-            return jnp.pad(low(v), ((0, 0), (0, 0), (0, 128 - v.shape[2])))
-        sm = jnp.concatenate(
-            [lanes(shifts), lanes(gains), lanes(mid_bias), jnp.zeros((LAYERS, 1, 128), F32), lanes(qv_bias[:, :, 0]),
-             jnp.zeros((LAYERS, 6, 128), F32)], axis=1)
+        small_in = (shifts, gains, mid_bias, qv_bias[:, :, 0])
     else:
         wl = lax.all_gather(wl, axes, axis=1, tiled=True)
         sh = lax.all_gather(shifts.astype(BF), axes, axis=2, tiled=True).astype(F32)
@@ -795,24 +916,11 @@
         kvb = jnp.concatenate([gap, bv[..., 0:128], gap, gap, bv[..., 128:192]], axis=2)
         fit = lambda v: jnp.pad(v, ((0, 0), (0, 0), (0, DM - v.shape[2])))
         sm = jnp.concatenate([sh, ga, mb, fit(bq), fit(kvb), jnp.zeros((LAYERS, 7, DM), F32)], axis=1)
-
-    nblk = length // BLK
-    nb = TL // BLK
-    seg = segment_ids[0]
-    segk = jnp.broadcast_to(seg[:, None], (length, 128))
-    rnd = lax.dynamic_slice_in_dim(random_blocks[0], z * nb, nb, axis=1)
-    qi = (z * nb + jnp.arange(nb, dtype=jnp.int32))[None, :, None]
-    kj = jnp.arange(nblk, dtype=jnp.int32)[None, None, :]
-    ok = (jnp.abs(qi - kj) <= 1) | (kj == 0) | (kj == nblk - 1)
-    ok = ok | jnp.any(rnd[:, :, :, None] == kj[:, :, None, :], axis=2)
-    segq = lax.dynamic_slice_in_dim(seg, z * TL, TL)
-    heads = rnd.shape[0]
-    segqm = jnp.where(ok.transpose(0, 2, 1)[:, :, :, None], segq.reshape(1, 1, nb, BLK), -1).reshape(heads, nblk, TL)
+        small_in = (sm,)
 
     QT = TL // 4
     L = LAYERS
     nslot = dp * nz if direct else 1
-    grw = rw if direct else DM
     vm = pl.BlockSpec(memory_space=pltpu.VMEM)
     dma = pltpu.SemaphoreType.DMA
     xr = nz * rw if direct else 16
@@ -857,6 +965,10 @@
         pltpu.VMEM((L, 8, DM), F32),
         pltpu.VMEM((nz - 1, L, 8, DM), F32),
         pltpu.VMEM((L, 8, DM), F32),
+        pltpu.VMEM((L, 16, 128), F32),
+        pltpu.VMEM((length, 128), F32),
+        pltpu.VMEM((3, length // BLK, TL), F32),
+        pltpu.VMEM((rw, DM) if direct else (8, 128), F32),
         dma((7, 5 + nz)), dma((7, 2 * nz)),
         dma((L, 5 * nz)), dma((L, 4 * nz)),
         dma((8, 6)), dma((8, 6)),
@@ -865,25 +977,40 @@
         dma((6, 2 * nz)), dma((6, 2 * nz)),
         dma((2 + nz,)), dma((2 + nz,)),
     ]
-    act, dx, gout, gsm = pl.pallas_call(
-        functools.partial(body, direct, nz, rw),
-        out_shape=(
-            jax.ShapeDtypeStruct((TL, DM), BF),
-            jax.ShapeDtypeStruct((TL, DM), BF),
-            jax.ShapeDtypeStruct((3 * L, grw, DM), F32 if direct else BF),
-            jax.ShapeDtypeStruct((L, 8, DM), F32),
-        ),
-        in_specs=[vm] * 6,
-        out_specs=(vm,) * 4,
+    tokens = (jax.ShapeDtypeStruct((TL, DM), BF), jax.ShapeDtypeStruct((TL, DM), F32))
+    if direct:
+        grads = [(L, 3, rw, 192), (L, rw, 192), (L, rw, DM), (L, rw, DM), (L, 24, 128)]
+        out_shape = tokens + tuple(jax.ShapeDtypeStruct(g, F32) for g in grads)
+    else:
+        out_shape = tokens + (jax.ShapeDtypeStruct((3 * L, DM, DM), BF), jax.ShapeDtypeStruct((L, 8, DM), F32))
+    args = (wl, x_in[0], cotangent[0], segment_ids, random_blocks[0]) + small_in
+    results = pl.pallas_call(
+        functools.partial(body, direct, nz, rw, len(args)),
+        out_shape=out_shape,
+        in_specs=[vm] * 4 + [pl.BlockSpec(memory_space=pltpu.SMEM)] + [vm] * len(small_in),
+        out_specs=(vm,) * len(out_shape),
         scratch_shapes=scratch,
         compiler_params=pltpu.CompilerParams(collective_id=0, has_side_effects=True, vmem_limit_bytes=60 * 2**20),
         name="encoder",
-    )(wl, sm, x_in[0], cotangent[0], segk, segqm)
-
-    if not direct:
-        gout = lax.psum_scatter(gout.astype(F32), axes, scatter_dimension=1, tiled=True)
-        gsm = lax.psum(gsm, "dp")
-    gout = gout.reshape(L, 3, rw, DM)
+    )(*args)
+    act, dx = results[:2]
+    if direct:
+        gq, go, g1, g2, gsm = results[2:]
+        return (
+            act[None],
+            dx[None],
+            gq.transpose(0, 2, 1, 3),
+            go.transpose(0, 2, 1),
+            g1,
+            g2.transpose(0, 2, 1),
+            gsm[:, 15:24:8, None, : rw // 4],
+            gsm[:, 6:7, :rw],
+            gsm[:, 0:4, :rw],
+            gsm[:, 4:6, :rw],
+        )
+    gout, gsm = results[2:]
+    gout = lax.psum_scatter(gout.astype(F32), axes, scatter_dimension=1, tiled=True).reshape(L, 3, rw, DM)
+    gsm = lax.psum(gsm, "dp")
     ga, g1, g2 = gout[:, 0], gout[:, 1], gout[:, 2]
     pc = [ga[:, :, i * 64 : (i + 1) * 64] for i in range(12)]
     gq = jnp.concatenate([pc[6], pc[7], pc[8]], axis=2)
@@ -896,7 +1023,7 @@
     qv = lax.dynamic_slice_in_dim(jnp.stack([dbq, dbv], axis=1), slot * (rw // 4), rw // 4, axis=2)
     return (
         act[None],
-        dx[None].astype(F32),
+        dx[None],
         jnp.stack([gq, gk, gv], axis=2),
         go,
         g1,

time: 316 us -> 301 us (0.953)
  Pallas kernels: 289 us -> 280 us
    pallas_call x1, Pallas kernels: 289 us -> 280 us  [shards(): pl.pallas_call(functools.partial(body, direct, nz, rw, len(args)), out_sh...]
    unnamed x43 -> x38, local copies, waits for them, and re-layouts: 4.56 us -> 10.1 us
where the time goes in v3:
time: 301 us; the launch traced here: 299 us
  Pallas kernels  280 us (93%)
  local copies, waits for them, and re-layouts  17.8 us (6%)
    pallas_call x1, Pallas kernels, shards(): pl.pallas_call(functools.partial(body, direct, nz, rw, len(args)), out_sh...  280 us
    unnamed x38, local copies, waits for them, and re-layouts  10.1 us

profile of v3, /device:TPU:0, one launch (start us, length us, event | category | flops | bytes accessed | tf_op | source)
XLA Modules:
  0.0 299.3 jit_solution(100548303181627815)
XLA Ops:
  0.6 0.0 copy-start.6
  0.7 1.2 fusion
  1.8 0.1 copy.65
  2.0 0.1 copy.66
  2.1 0.0 copy-start.1
  2.1 0.1 copy.73
  2.2 0.1 copy.75
  2.4 0.1 copy.76
  2.5 0.1 copy.67
  2.6 0.0 copy-start.2
  2.6 0.1 copy.68
  2.7 0.1 copy.69
  2.9 0.1 copy.70
  3.0 0.1 copy.71
  3.1 0.1 copy.72
  3.2 0.1 copy.74
  3.3 0.0 copy-done.6
  3.4 0.1 copy.77
  3.5 0.1 copy.78
  3.6 0.1 copy.79
  3.7 0.2 concatenate.4
  3.9 0.0 copy-done.1
  4.0 0.0 copy-done.2
  4.0 0.0 copy-start.7
  4.1 0.1 pad_maximum_fusion
  4.2 1.0 copy.61
  5.1 0.0 copy-done.7
  5.1 0.7 copy.62
  5.9 280.2 %encoder.1 = (bf16[512,768]{1,0:T(8,128)(2,1)}, f32[512,768]{1,0:T(8,128)}, f32[2,3,96,192]{3,2,1,0:T(8,128)}, f32[2,96,192]{2,1,0:T(8,128)}, f32[2,96,768]{2,1,...) custom-call(bf16[6,96,768]{2,1,0:T(8,128)(2,1)} %bitcast.38, bf16[512,768]{1,0:T(8,128)(2,1)} %bitcast.42, ...), custom_call_target="tpu_custom_call" | custom-call | tf_op jit(solution)/shard_map/encoder/pallas_call | solution.py:987
  286.0 0.0 copy-start
  286.0 1.4 slice.86
  287.5 1.3 slice.84
  288.8 1.3 slice.87
  290.0 1.3 slice.85
  291.3 1.7 copy.63
  293.0 2.1 copy.85
  295.1 0.0 copy-done
  295.1 0.0 copy-start.5
  295.1 0.0 copy-start.4
  295.1 1.1 copy.86
  296.2 0.3 copy-done.5
  296.5 0.0 copy-start.3
  296.5 0.8 copy.87
  297.4 0.0 copy-done.4
  297.4 0.8 copy.88
  298.2 0.0 copy-done.3
  298.2 0.8 copy.89
  (7 shorter events, 0.1 us)
Async XLA Ops:
  0.6 2.7 copy-start.6
  2.1 1.9 copy-start.1
  2.6 1.4 copy-start.2
  4.0 1.1 copy-start.7
  286.0 9.1 %copy-start = (f32[512,768]{1,0:T(8,128)S(1)}, f32[512,768]{1,0:T(8,128)}, u32[]{:S(2)}) copy-start(f32[512,768]{1,0:T(8,128)} %get-tuple-element.18) | copy-start | bytes 4718596
  295.1 1.4 copy-start.5
  295.1 2.3 copy-start.4
  296.5 1.6 copy-start.3

commit v4 on v3

--- a/solution.py
+++ b/solution.py
@@ -49,8 +49,8 @@
     ins, refs = refs[:n_in], refs[n_in:]
     if direct:
         wl, xin, cot, seg, rnd, sh_in, ga_in, mb_in, qv_in = ins
-        act, dxo, gq_out, go_out, g1_out, g2_out, gsm = refs[:7]
-        refs = refs[7:]
+        act, dxo, gq_out, go_out, g1_out, g2_out, qv_out, mb_out, sh_out, ga_out = refs[:10]
+        refs = refs[10:]
     else:
         wl, xin, cot, seg, rnd, sm = ins
         act, dxo, gout, gsm = refs[:4]
@@ -791,10 +791,10 @@
         EB[0, own_part(b), :] = v.astype(BF)
 
     forward(1, [
-        run((w_b, 4), (w_a, 5)),
+        run((w_b, 4)),
         run((w_c, 4)),
         run((w_d, 4)),
-        run(),
+        run((w_a, 5)),
         run((w_b, 5)),
         run((w_c, 5), (w_d, 5)),
         run(),
@@ -817,7 +817,7 @@
         for b in range(2):
             lower[0](b, dy[b * ST : (b + 1) * ST])
 
-    backward(1, {0: run((act_start,)), 1: run((act_end,)), 3: run((g_mid, 5)), 4: run((g_add, 5)), 5: run((g_mid, 4))}, done, gone, to_lower)
+    backward(1, {0: run((act_start,)), 1: run((act_end,)), 3: run((g_mid, 5)), 4: run((g_add, 5)), 5: nop}, done, gone, to_lower)
 
     keep = lax.broadcasted_iota(jnp.int32, SL.shape, 1) < 6
 
@@ -837,7 +837,7 @@
         dx_put(1)
 
     backward(
-        0, {1: run((g_add, 4), (g_mid, 3), (g_fin, 5)), 3: run((g_add, 3), (g_mid, 2), (g_fin, 4)), 4: run((g_add, 2)), 5: run((s1,), (g_mid, 1), (g_fin, 3))}, lower[1], lower[2], to_output
+        0, {0: run((g_mid, 4)), 1: run((g_add, 4), (g_mid, 3), (g_fin, 5)), 3: run((g_add, 3), (g_mid, 2), (g_fin, 4)), 4: run((g_add, 2)), 5: run((s1,), (g_mid, 1), (g_fin, 3))}, lower[1], lower[2], to_output
     )
 
     sc[0].wait_recv()
@@ -870,12 +870,15 @@
         lane = lax.broadcasted_iota(jnp.int32, (8, DM), 1)
         for l in range(LAYERS):
             x = tot[l]
-            gsm[l, 0:8, :] = pltpu.roll(x, lax.rem(DM - slot * rw, DM), 1)[:, 0:128]
+            own_cols = pltpu.roll(x, lax.rem(DM - slot * rw, DM), 1)
+            sh_out[l] = own_cols[0:4, 0:rw]
+            ga_out[l] = own_cols[4:6, 0:rw]
+            mb_out[l] = own_cols[6:7, 0:rw]
             gq = pltpu.roll(x, DM - 384, 1)
             gv = jnp.where(lane < 128, pltpu.roll(x, DM - 64, 1), pltpu.roll(x, DM - 192, 1))
             back = lax.rem(DM - slot * (rw // 4), DM)
-            gsm[l, 8:16, :] = pltpu.roll(gq, back, 1)[:, 0:128]
-            gsm[l, 16:24, :] = pltpu.roll(gv, back, 1)[:, 0:128]
+            qv_out[l, 0:1, :] = pltpu.roll(gq, back, 1)[7:8, 0 : rw // 4]
+            qv_out[l, 1:2, :] = pltpu.roll(gv, back, 1)[7:8, 0 : rw // 4]
     else:
         gsm[...] = tot
     g_fin(0)
@@ -979,7 +982,7 @@
     ]
     tokens = (jax.ShapeDtypeStruct((TL, DM), BF), jax.ShapeDtypeStruct((TL, DM), F32))
     if direct:
-        grads = [(L, 3, rw, 192), (L, rw, 192), (L, rw, DM), (L, rw, DM), (L, 24, 128)]
+        grads = [(L, 3, rw, 192), (L, rw, 192), (L, rw, DM), (L, rw, DM), (L, 2, rw // 4), (L, 1, rw), (L, 4, rw), (L, 2, rw)]
         out_shape = tokens + tuple(jax.ShapeDtypeStruct(g, F32) for g in grads)
     else:
         out_shape = tokens + (jax.ShapeDtypeStruct((3 * L, DM, DM), BF), jax.ShapeDtypeStruct((L, 8, DM), F32))
@@ -995,7 +998,7 @@
     )(*args)
     act, dx = results[:2]
     if direct:
-        gq, go, g1, g2, gsm = results[2:]
+        gq, go, g1, g2, gqv, gmid, gsh, gga = results[2:]
         return (
             act[None],
             dx[None],
@@ -1003,10 +1006,10 @@
             go.transpose(0, 2, 1),
             g1,
             g2.transpose(0, 2, 1),
-            gsm[:, 15:24:8, None, : rw // 4],
-            gsm[:, 6:7, :rw],
-            gsm[:, 0:4, :rw],
-            gsm[:, 4:6, :rw],
+            gqv[:, :, None, :],
+            gmid,
+            gsh,
+            gga,
         )
     gout, gsm = results[2:]
     gout = lax.psum_scatter(gout.astype(F32), axes, scatter_dimension=1, tiled=True).reshape(L, 3, rw, DM)

time: 301 us -> 297 us (0.987)
  local copies, waits for them, and re-layouts: 17.8 us -> 14.6 us
    slice x4 -> x0, local copies, waits for them, and re-layouts: 5.25 us -> none  [the longest x1 1.41 us: shards(): gsm[:, 0:4, :rw]]
    pallas_call x1, Pallas kernels: 280 us -> 277 us  [shards(): pl.pallas_call(functools.partial(body, direct, nz, rw, len(args)), out_sh...]
    unnamed x38 -> x46, local copies, waits for them, and re-layouts: 10.1 us -> 13.3 us
where the time goes in v4:
time: 297 us; the launch traced here: 294 us
  Pallas kernels  277 us (93%)
  local copies, waits for them, and re-layouts  14.6 us (5%)
    pallas_call x1, Pallas kernels, shards(): pl.pallas_call(functools.partial(body, direct, nz, rw, len(args)), out_sh...  277 us
    unnamed x46, local copies, waits for them, and re-layouts  13.3 us

profile of v4, /device:TPU:0, one launch (start us, length us, event | category | flops | bytes accessed | tf_op | source)
XLA Modules:
  0.0 294.4 jit_solution(15017549632325219656)
XLA Ops:
  0.6 0.0 copy-start.1
  0.7 0.0 copy-start.5
  0.7 1.5 copy.62
  2.2 0.9 convert.65
  3.1 0.1 copy.79
  3.2 0.1 copy.78
  3.3 0.1 copy.77
  3.5 1.1 convert_bitcast_fusion.1
  4.6 0.0 copy-done.1
  4.6 0.0 copy-done.5
  4.7 0.1 copy.73
  4.8 0.1 copy.76
  4.9 0.1 copy.75
  5.0 0.1 copy.74
  5.1 0.1 copy.67
  5.3 0.1 copy.72
  5.4 0.1 copy.69
  5.5 0.1 copy.68
  5.6 0.1 copy.65
  5.8 0.1 copy.71
  5.9 0.1 copy.70
  6.0 0.1 copy.66
  6.1 0.2 concatenate.4
  6.4 0.1 pad_maximum_fusion
  6.5 1.0 copy.61
  7.4 276.5 %encoder.1 = (bf16[512,768]{1,0:T(8,128)(2,1)}, f32[512,768]{1,0:T(8,128)}, f32[2,3,96,192]{3,2,1,0:T(8,128)}, f32[2,96,192]{2,1,0:T(8,128)}, f32[2,96,768]{2,1,...) custom-call(bf16[6,96,768]{2,1,0:T(8,128)(2,1)} %bitcast.38, ...), custom_call_target="tpu_custom_call" | custom-call | tf_op jit(solution)/shard_map/encoder/pallas_call | solution.py:990
  284.0 0.0 copy-start
  284.0 1.9 copy.63
  285.8 2.1 copy.89
  287.9 0.0 copy-done
  287.9 0.0 copy-start.4
  287.9 0.0 copy-start.3
  287.9 1.1 copy.90
  289.0 0.3 copy-done.4
  289.3 0.0 copy-start.2
  289.3 0.0 copy-start.8
  289.3 0.0 copy-start.9
  289.3 0.0 copy-start.6
  289.3 0.0 copy-start.7
  289.4 0.8 copy.91
  290.2 0.0 copy-done.3
  290.2 0.8 copy.92
  291.0 0.0 copy-done.2
  291.0 0.8 copy.93
  291.8 0.0 copy-done.8
  291.8 0.6 copy.94
  292.4 0.0 copy-done.9
  292.4 0.6 copy.95
  293.0 0.0 copy-done.6
  293.0 0.6 copy.96
  293.6 0.0 copy-done.7
  293.6 0.6 copy.97
  (6 shorter events, 0.1 us)
Async XLA Ops:
  0.6 3.9 %copy-start.1 = (f32[2,768,96]{1,2,0:T(8,128)S(1)}, f32[2,768,96]{1,2,0:T(8,128)}, u32[]{:S(2)}) copy-start(f32[2,768,96]{1,2,0:T(8,128)} %param.19) | copy-start | bytes 1769476
  0.7 4.0 %copy-start.5 = (f32[2,96,3,192]{3,1,2,0:T(8,128)S(1)}, f32[2,96,3,192]{3,1,2,0:T(8,128)}, u32[]{:S(2)}) copy-start(f32[2,96,3,192]{3,1,2,0:T(8,128)} %param.16) | copy-start | bytes 1327108
  284.0 3.9 %copy-start = (f32[512,768]{1,0:T(8,128)S(1)}, f32[512,768]{1,0:T(8,128)}, u32[]{:S(2)}) copy-start(f32[512,768]{1,0:T(8,128)} %get-tuple-element.21) | copy-start | bytes 4718596
  287.9 1.4 copy-start.4
  287.9 2.3 copy-start.3
  289.3 1.7 copy-start.2
  289.3 2.5 copy-start.8
  289.3 3.1 %copy-start.9 = (f32[2,1,96]{2,1,0:T(1,128)S(1)}, f32[2,1,96]{2,1,0:T(1,128)}, u32[]{:S(2)}) copy-start(f32[2,1,96]{2,1,0:T(1,128)} %get-tuple-element.92) | copy-start | bytes 2308
  289.3 3.6 %copy-start.6 = (f32[2,4,96]{2,1,0:T(4,128)S(1)}, f32[2,4,96]{2,1,0:T(4,128)}, u32[]{:S(2)}) copy-start(f32[2,4,96]{2,1,0:T(4,128)} %get-tuple-element.93) | copy-start | bytes 9220
  289.3 4.2 %copy-start.7 = (f32[2,2,96]{2,1,0:T(2,128)S(1)}, f32[2,2,96]{2,1,0:T(2,128)}, u32[]{:S(2)}) copy-start(f32[2,2,96]{2,1,0:T(2,128)} %get-tuple-element.94) | copy-start | bytes 4612
